TPU v7x, 32 devices: a whole 2x2x4 slice. The times are simulated.
32 devices in a mesh: ctx: 4 (over y, x), mem: 8 (over z, core).
Axes of the slice: x: 2, y: 2, z: 4, core: 2. Of those that a mesh axis runs over, the one named last changes fastest.
Arguments:
- queries: bfloat16 [1536, 4096], P('ctx', 'mem'), may hold values from -6 to 6
- keys: bfloat16 [1536, 4096], P('ctx', 'mem'), may hold values from -6 to 6
- values: bfloat16 [1536, 4096], P('ctx', 'mem'), may hold values from -6 to 6
- out_grad: bfloat16 [1536, 4096], P('ctx', 'mem'), may hold values from -6 to 6
- mem_keys: bfloat16 [1024, 4096], P('mem'), may hold values from -6 to 6
- mem_values: bfloat16 [1024, 4096], P('mem'), may hold values from -6 to 6
- gate_logit: float32 [32], P('mem'), may hold values from -3 to 3
- block_ids: int32 [12, 4], P('ctx'), may hold values from 0 to 7, all different within a row
Outputs:
- mixed: bfloat16 [1536, 4096], P('ctx', 'mem')
- query_grad: bfloat16 [1536, 4096], P('ctx', 'mem')
- mem_key_grad: bfloat16 [1024, 4096], P('mem', 'ctx')
- mem_value_grad: bfloat16 [1024, 4096], P('mem', 'ctx')
Inputs may be any that keep to these rules, and one draw needn't show every extreme that they name: `block_ids`: the 4 ids listed for one query block are distinct, and every memory block is listed somewhere.
All inputs are finite; a program needn't handle non-finite values.
Results may differ from a plain program's by a relative error of at most 0.02.
Values may be sent and summed in bfloat16 or wider, within the bound.
A program may use at most 64 MiB of HBM per device.

v0:
```python
import jax
import jax.numpy as jnp
from jax import lax
from jax.sharding import PartitionSpec as P

HEAD_SIZE = 128
BLOCK = 128


def shards(queries, keys, values, out_grad, mem_keys, mem_values, gate_logit, block_ids):
    tok_count = queries.shape[0]
    columns = queries.shape[1]
    head_count = columns // HEAD_SIZE
    scores_scale_factor = HEAD_SIZE ** (-0.5)
    query_start = lax.axis_index("ctx") * tok_count
    query_heads = queries.reshape(tok_count, head_count, HEAD_SIZE)
    query_pos = query_start + jnp.arange(tok_count, dtype=jnp.int32)
    gate_share = jax.nn.sigmoid(gate_logit)[None, :, None]

    def causal_scores(shard_keys):
        row_count = shard_keys.shape[0]
        scores = (
            jnp.einsum(
                "qhd,khd->hqk",
                query_heads,
                shard_keys.reshape(row_count, head_count, HEAD_SIZE),
                preferred_element_type=jnp.float32,
            )
            * scores_scale_factor
        )
        key_pos = jnp.arange(row_count, dtype=jnp.int32)
        causal = (key_pos[None, :] <= query_pos[:, None])[None]
        return (jnp.where(causal, scores, -1e30), causal)

    run_max = jnp.full((head_count, tok_count), -1e30, jnp.float32)
    shard_keys = lax.all_gather(keys, "ctx", axis=0, tiled=True)
    shard_values = lax.all_gather(values, "ctx", axis=0, tiled=True)
    row_count = shard_keys.shape[0]
    masked, causal = causal_scores(shard_keys)
    new_max = jnp.maximum(run_max, jnp.max(masked, axis=-1))
    weights = jnp.where(causal, jnp.exp(masked - new_max[..., None]), 0.0)
    run_total = jnp.sum(weights, axis=-1)
    run_acc = jnp.einsum(
        "hqk,khd->hqd",
        weights.astype(jnp.bfloat16),
        shard_values.reshape(row_count, head_count, HEAD_SIZE),
        preferred_element_type=jnp.float32,
    )
    run_max, run_total, run_acc = (new_max, run_total, run_acc)
    local_out = (run_acc / run_total[..., None]).transpose(1, 0, 2)
    log_total = run_max + jnp.log(run_total)
    fetched_keys, fetched_values = (
        lax.all_to_all(mem_keys, "mem", split_axis=1, concat_axis=0, tiled=True),
        lax.all_to_all(mem_values, "mem", split_axis=1, concat_axis=0, tiled=True),
    )
    block_count = fetched_keys.shape[0] // BLOCK
    query_block_list = tok_count // BLOCK
    list_len = block_ids.shape[1]
    selected_keys = fetched_keys.reshape(block_count, BLOCK, columns)[block_ids].reshape(
        query_block_list, list_len * BLOCK, head_count, HEAD_SIZE
    )
    selected_values = fetched_values.reshape(block_count, BLOCK, columns)[block_ids].reshape(
        query_block_list, list_len * BLOCK, head_count, HEAD_SIZE
    )
    block_queries = queries.reshape(query_block_list, BLOCK, head_count, HEAD_SIZE)
    memory_score_matrix = (
        jnp.einsum(
            "bqhd,bkhd->bhqk", block_queries, selected_keys, preferred_element_type=jnp.float32
        )
        * scores_scale_factor
    )
    weights = jax.nn.softmax(memory_score_matrix, axis=-1)
    weights_reduced = weights.astype(jnp.bfloat16)
    memory_output = jnp.einsum(
        "bhqk,bkhd->bqhd", weights_reduced, selected_values, preferred_element_type=jnp.float32
    )
    mem_flat = memory_output.reshape(tok_count, head_count, HEAD_SIZE)
    mixed = (
        (gate_share * mem_flat + (1.0 - gate_share) * local_out)
        .reshape(tok_count, columns)
        .astype(jnp.bfloat16)
    )
    grad_full = out_grad.reshape(tok_count, head_count, HEAD_SIZE).astype(jnp.float32)
    grad_mem = gate_share * grad_full
    grad_local = (1.0 - gate_share) * grad_full
    grad_local_low = grad_local.astype(jnp.bfloat16)
    local_delta = jnp.sum(grad_local * local_out, axis=-1).T
    shard_keys = lax.all_gather(keys, "ctx", axis=0, tiled=True)
    shard_values = lax.all_gather(values, "ctx", axis=0, tiled=True)
    row_count = shard_keys.shape[0]
    masked, causal = causal_scores(shard_keys)
    probs = jnp.where(causal, jnp.exp(masked - log_total[..., None]), 0.0)
    grad_probs = jnp.einsum(
        "qhd,khd->hqk",
        grad_local_low,
        shard_values.reshape(row_count, head_count, HEAD_SIZE),
        preferred_element_type=jnp.float32,
    )
    grad_scores = probs * (grad_probs - local_delta[..., None])
    local_grad = (
        jnp.einsum(
            "hqk,khd->qhd",
            grad_scores.astype(jnp.bfloat16),
            shard_keys.reshape(row_count, head_count, HEAD_SIZE),
            preferred_element_type=jnp.float32,
        )
        * scores_scale_factor
    )
    grad_mem_blocks = grad_mem.reshape(query_block_list, BLOCK, head_count, HEAD_SIZE)
    memory_gradient_reduced = grad_mem_blocks.astype(jnp.bfloat16)
    weight_gradient = jnp.einsum(
        "bqhd,bkhd->bhqk",
        memory_gradient_reduced,
        selected_values,
        preferred_element_type=jnp.float32,
    )
    mem_delta = jnp.sum(grad_mem_blocks * memory_output, axis=-1).transpose(0, 2, 1)
    memory_score_gradient = (weights * (weight_gradient - mem_delta[..., None])).astype(
        jnp.bfloat16
    )
    memory_gradient = (
        jnp.einsum(
            "bhqk,bkhd->bqhd",
            memory_score_gradient,
            selected_keys,
            preferred_element_type=jnp.float32,
        )
        * scores_scale_factor
    )
    query_grad = (
        (memory_gradient.reshape(tok_count, head_count, HEAD_SIZE) + local_grad)
        .reshape(tok_count, columns)
        .astype(jnp.bfloat16)
    )
    selected_key_gradient = (
        jnp.einsum(
            "bhqk,bqhd->bkhd",
            memory_score_gradient,
            block_queries,
            preferred_element_type=jnp.float32,
        )
        * scores_scale_factor
    )
    selected_value_gradient = jnp.einsum(
        "bhqk,bqhd->bkhd",
        weights_reduced,
        memory_gradient_reduced,
        preferred_element_type=jnp.float32,
    )
    one_hot = (
        block_ids.reshape(-1)[:, None] == jnp.arange(block_count, dtype=jnp.int32)[None, :]
    ).astype(jnp.float32)
    part_keys = jnp.einsum(
        "jb,jrc->brc",
        one_hot,
        selected_key_gradient.reshape(query_block_list * list_len, BLOCK, columns),
        precision=lax.Precision.HIGHEST,
    ).reshape(block_count * BLOCK, columns)
    part_values = jnp.einsum(
        "jb,jrc->brc",
        one_hot,
        selected_value_gradient.reshape(query_block_list * list_len, BLOCK, columns),
        precision=lax.Precision.HIGHEST,
    ).reshape(block_count * BLOCK, columns)
    keys_low = part_keys.astype(jnp.bfloat16)
    values_low = part_values.astype(jnp.bfloat16)
    owner_keys, owner_values = (
        lax.all_to_all(keys_low, "mem", split_axis=0, concat_axis=1, tiled=True),
        lax.all_to_all(values_low, "mem", split_axis=0, concat_axis=1, tiled=True),
    )
    summed_keys, summed_values = (
        lax.psum_scatter(
            owner_keys.astype(jnp.float32).astype(jnp.bfloat16),
            "ctx",
            scatter_dimension=1,
            tiled=True,
        ).astype(jnp.float32),
        lax.psum_scatter(
            owner_values.astype(jnp.float32).astype(jnp.bfloat16),
            "ctx",
            scatter_dimension=1,
            tiled=True,
        ).astype(jnp.float32),
    )
    return (mixed, query_grad, summed_keys.astype(jnp.bfloat16), summed_values.astype(jnp.bfloat16))


def solution(mesh):
    in_specs = (
        P("ctx", "mem"),
        P("ctx", "mem"),
        P("ctx", "mem"),
        P("ctx", "mem"),
        P("mem", None),
        P("mem", None),
        P("mem"),
        P("ctx", None),
    )
    out_specs = (P("ctx", "mem"), P("ctx", "mem"), P("mem", "ctx"), P("mem", "ctx"))
    return jax.shard_map(shards, mesh=mesh, in_specs=in_specs, out_specs=out_specs, check_vma=False)
```

profile of v0, /device:TPU:3, one launch (start us, length us, event | category | flops | bytes accessed | tf_op | source)
XLA Modules:
  0.0 183.3 jit_solution(13207902592807852779)
XLA Ops:
  7.9 1.7 copy.122
  9.6 1.3 copy.123
  11.0 5.7 %all-to-all-start.1 = ((bf16[128,8,512]{2,0,1:T(8,128)(2,1)}), bf16[128,8,512]{2,0,1:T(8,128)(2,1)S(1)}, u32[]{:S(2)}, u32[]{:S(2)}) async-start(bf16[128,8,512]{2,0,1:T(8,128)(2,1)} %copy.123), calls=%async_computation.1 | async-start | bytes 2097152 | tf_op jit(solution)/shard_map/all_to_all | solution.py:53
  21.5 20.9 %all-to-all-done.1 = bf16[128,8,512]{2,0,1:T(8,128)(2,1)S(1)} async-done(((bf16[128,8,512]{2,0,1:T(8,128)(2,1)}), bf16[128,8,512]{2,0,1:T(8,128)(2,1)S(1)}, u32[]{:S(2)}, u32[]{:S(2)}) %all-to-all-start.1) | async-done | bytes 1048608 | tf_op jit(solution)/shard_map/all_to_all | solution.py:53
  42.4 5.0 %all-to-all-start = ((bf16[128,8,512]{2,0,1:T(8,128)(2,1)}), bf16[128,8,512]{2,0,1:T(8,128)(2,1)}, u32[]{:S(2)}, u32[]{:S(2)}) async-start(bf16[128,8,512]{2,0,1:T(8,128)(2,1)} %copy.121), calls=%async_computation | async-start | bytes 2097152 | tf_op jit(solution)/shard_map/all_to_all | solution.py:54
  49.6 2.7 %fusion.83 = (f32[3,4,128]{2,1,0:T(4,128)S(1)}, f32[3,4,128,512]{2,3,1,0:T(8,128)}) fusion(f32[3,4,512,128]{3,2,1,0:T(8,128)S(1)} %fusion.29), kind=kOutput, calls=%fused_computation.76 | output fusion | flops 3146239 | bytes 6297600 | tf_op jit(solution)/shard_map/sub | solution.py:72
  52.3 4.7 %convolution_bitcast_fusion = f32[3,512,4,128]{1,3,2,0:T(8,128)S(1)} fusion(f32[3,128,4,128]{3,2,1,0:T(4,128)} %reshape.121, f32[4]{0:T(128)} %get-tuple-element.25, f32[3,4,128]{2,1,0:T(4,128)S(1)} %get-tuple-element.30, f32[3,4,512,128]{3,2,1,0:T(8,128)} %copy-done.3), kind=kOutput, calls=%fused_computation.23 | convolution fusion | flops 205654016 | bytes 7084048 | tf_op jit(solution)/shard_map/bhqk,bqhd->bkhd/dot_general | solution.py:144
  57.0 2.9 %copy.151 = f32[3,512,4,128]{3,2,1,0:T(4,128)} copy(f32[3,512,4,128]{1,3,2,0:T(8,128)S(1)} %convolution_bitcast_fusion) | data formatting | bytes 6291456 | tf_op jit(solution)/shard_map/bhqk,bqhd->bkhd/transpose | solution.py:144
  59.9 3.3 %reshape.120 = f32[12,128,512]{2,1,0:T(8,128)S(1)} reshape(f32[3,512,4,128]{3,2,1,0:T(4,128)} %copy.151) | data formatting | bytes 6291456 | tf_op jit(solution)/shard_map/reshape | solution.py:162
  63.2 3.9 %fusion.20 = bf16[8,128,512]{2,0,1:T(8,128)(2,1)S(1)} fusion(f32[12,128,512]{2,1,0:T(8,128)S(1)} %reshape.120, s32[12]{0:T(128)} %eq.15), kind=kOutput, calls=%fused_computation.27 | convolution fusion | flops 76021856 | bytes 4194352 | tf_op jit(solution)/shard_map/jb,jrc->brc/dot_general | solution.py:159
  68.4 4.8 %all-to-all-done = bf16[128,8,512]{2,0,1:T(8,128)(2,1)} async-done(((bf16[128,8,512]{2,0,1:T(8,128)(2,1)}), bf16[128,8,512]{2,0,1:T(8,128)(2,1)}, u32[]{:S(2)}, u32[]{:S(2)}) %all-to-all-start) | async-done | bytes 1048608 | tf_op jit(solution)/shard_map/all_to_all | solution.py:54
  73.2 5.0 %all-to-all-start.3 = ((bf16[8,128,512]{2,1,0:T(8,128)(2,1)}), bf16[8,128,512]{2,1,0:T(8,128)(2,1)}, u32[]{:S(2)}, u32[]{:S(2)}) async-start(bf16[8,128,512]{2,1,0:T(8,128)(2,1)} %copy.153), calls=%async_computation.4 | async-start | bytes 2097152 | tf_op jit(solution)/shard_map/all_to_all | solution.py:169
  80.5 1.9 %gather_fusion = bf16[12,128,512]{2,1,0:T(8,128)(2,1)S(1)} fusion(bf16[8,128,512]{2,1,0:T(8,128)(2,1)} %bitcast.1, s32[1024]{0:T(1024)S(1)} %pad_clamp_fusion), kind=kCustom, calls=%fused_computation | custom fusion | bytes 3145776 | tf_op jit(solution)/shard_map/gather | solution.py:62
  82.4 1.9 %reshape.111 = bf16[3,512,4,128]{3,2,1,0:T(4,128)(2,1)} reshape(bf16[12,128,512]{2,1,0:T(8,128)(2,1)S(1)} %gather_fusion) | data formatting | bytes 3145728 | tf_op jit(solution)/shard_map/reshape | solution.py:62
  84.2 6.7 %multiply_reduce_fusion.1 = (f32[3,128,4]{1,2,0:T(4,128)}, f32[3,128,4,128]{3,1,2,0:T(8,128)}) fusion(f32[3,128,4,128]{3,2,1,0:T(4,128)} %reshape.121, f32[4]{0:T(128)S(1)} %copy-done.21, f32[3,4,128]{2,1,0:T(4,128)S(1)} %get-tuple-element.30, f32[3,4,512,128]{3,2,1,0:T(8,128)} %copy-done.3, bf16[3,512,4,128]{3,2,1,0:T(4,128)(2,1)} %reshape.111), kind=kOutput, calls=%fused_computation.48 | convolution fusion | flops 205849088 | bytes 6303760 | tf_op jit(solution)/shard_map/bhqk,bkhd->bqhd/dot_general | solution.py:74
  90.9 2.4 %multiply_convert_fusion.1 = bf16[3,4,128,512]{2,3,1,0:T(8,128)(2,1)S(1)} fusion(f32[3,4,128]{2,1,0:T(4,128)} %bitcast.105, bf16[3,512,4,128]{3,2,1,0:T(4,128)(2,1)} %reshape.111, f32[3,4,128,512]{2,3,1,0:T(8,128)S(1)} %copy-done.7, f32[3,4,128]{2,1,0:T(4,128)S(1)} %get-tuple-element.30, f32[3,128,4,128]{3,2,1,0:T(4,128)} %reshape.121, f32[4]{0:T(128)S(1)} %copy-done.21), kind=kOutput, calls=%fused_computation.20 | convolution fusion | flops 204865536 | bytes 7090192 | tf_op jit(solution)/shard_map/bqhd,bkhd->bhqk/dot_general | solution.py:111
  95.0 3.7 %copy.145 = f32[3,512,4,128]{3,2,1,0:T(4,128)} copy(f32[3,512,4,128]{3,1,2,0:T(8,128)S(1)} %multiply_bitcast_fusion) | data formatting | bytes 6291456 | tf_op jit(solution)/shard_map/mul | solution.py:136
  98.7 3.3 %reshape.119 = f32[12,128,512]{2,1,0:T(8,128)S(1)} reshape(f32[3,512,4,128]{3,2,1,0:T(4,128)} %copy.145) | data formatting | bytes 6291456 | tf_op jit(solution)/shard_map/reshape | solution.py:156
  102.1 3.3 %fusion.17 = bf16[8,128,512]{2,0,1:T(8,128)(2,1)S(1)} fusion(f32[12,128,512]{2,1,0:T(8,128)S(1)} %reshape.119, s32[12]{0:T(128)S(1)} %copy-done.18), kind=kOutput, calls=%fused_computation.26 | convolution fusion | flops 76021856 | bytes 4194352 | tf_op jit(solution)/shard_map/jb,jrc->brc/dot_general | solution.py:153
  106.6 5.4 %all-to-all-start.2 = ((bf16[8,128,512]{2,1,0:T(8,128)(2,1)}), bf16[8,128,512]{2,1,0:T(8,128)(2,1)}, u32[]{:S(2)}, u32[]{:S(2)}) async-start(bf16[8,128,512]{2,1,0:T(8,128)(2,1)} %copy.147), calls=%async_computation.2 | async-start | bytes 2097152 | tf_op jit(solution)/shard_map/all_to_all | solution.py:168
  112.0 2.3 %copy.154 = bf16[8,128,512]{1,2,0:T(8,128)(2,1)} copy(bf16[8,128,512]{2,1,0:T(8,128)(2,1)} %all-to-all-done.3) | data formatting | bytes 2097152 | tf_op jit(solution)/shard_map/all_to_all | solution.py:169
  117.8 2.6 %copy.133 = bf16[1536,512]{0,1:T(8,128)(2,1)} copy(bf16[1536,512]{1,0:T(8,128)(2,1)} %all-gather.5.cloned.1.call-done) | data formatting | bytes 3145728 | tf_op jit(solution)/shard_map/all_gather | solution.py:37
  120.4 3.4 %fusion.3 = (f32[4,384]{1,0:T(4,128)S(1)}, f32[4,384,1536]{2,1,0:T(8,128)S(1)}) fusion(pred[384,1536]{1,0:T(8,128)(4,1)S(1)} %copy-done.6, bf16[1536,4,128]{0,2,1:T(8,128)(2,1)} %bitcast.96, bf16[384,512]{1,0:T(8,128)(2,1)S(1)} %copy-done.9), kind=kOutput, calls=%fused_computation.8 | convolution fusion | flops 611056128 | bytes 11999232 | tf_op jit(solution)/shard_map/qhd,khd->hqk/dot_general | solution.py:23
  123.8 3.1 %fusion.1 = f32[4,384]{1,0:T(4,128)S(1)} fusion(f32[4,384,1536]{2,1,0:T(8,128)S(1)} %get-tuple-element.29, f32[4,384]{1,0:T(4,128)S(1)} %broadcast_maximum_fusion, pred[384,1536]{1,0:T(8,128)(4,1)S(1)} %copy-done.6), kind=kLoop, calls=%fused_computation.6 | loop fusion | flops 11794944 | bytes 10039296 | tf_op jit(solution)/shard_map/reduce_sum | solution.py:42
  127.4 10.4 %all-to-all-done.2 = bf16[8,128,512]{2,1,0:T(8,128)(2,1)} async-done(((bf16[8,128,512]{2,1,0:T(8,128)(2,1)}), bf16[8,128,512]{2,1,0:T(8,128)(2,1)}, u32[]{:S(2)}, u32[]{:S(2)}) %all-to-all-start.2) | async-done | bytes 1048608 | tf_op jit(solution)/shard_map/all_to_all | solution.py:168
  137.8 2.3 %copy.148 = bf16[8,128,512]{1,2,0:T(8,128)(2,1)} copy(bf16[8,128,512]{2,1,0:T(8,128)(2,1)} %all-to-all-done.2) | data formatting | bytes 2097152 | tf_op jit(solution)/shard_map/all_to_all | solution.py:168
  140.2 7.5 %multiply_reduce_fusion = (f32[384,4]{0,1:T(4,128)S(1)}, bf16[384,4,128]{0,2,1:T(8,128)(2,1)S(1)}) fusion(f32[384,512]{0,1:T(8,128)S(1)} %copy-done.14, f32[4]{0:T(128)S(1)} %copy-done.20, f32[384,4,128]{0,2,1:T(8,128)} %copy.129, f32[4]{0:T(128)S(1)} %copy-done.21, f32[384,4]{0,1:T(4,128)S(1)} %bitcast.103, bf16[1536,4,128]{0,2,1:T(8,128)(2,1)} %bitcast.98, ...), kind=kOutput, calls=%fused_computation.47 | convolution fusion | flops 617347584 | bytes 13584416 | tf_op jit(solution)/shard_map/hqk,khd->hqd/dot_general | solution.py:43
  147.7 9.6 %fusion.47 = bf16[384,4,128]{0,2,1:T(8,128)(2,1)} fusion(f32[384,4,128]{0,2,1:T(8,128)} %copy.143, bf16[1536,4,128]{0,2,1:T(8,128)(2,1)S(1)} %bitcast.97, f32[4,384,1536]{2,1,0:T(8,128)} %copy-done, bf16[1536,4,128]{0,2,1:T(8,128)(2,1)} %bitcast.99, f32[4,384]{1,0:T(4,128)S(1)} %bitcast.104, f32[4,384]{1,0:T(4,128)S(1)} %log_add_fusion, ...), kind=kOutput, calls=%fused_computation.44 | convolution fusion | flops 1225457664 | bytes 15151120 | tf_op jit(solution)/shard_map/hqk,khd->qhd/dot_general | solution.py:101
  157.3 1.9 %copy.156 = bf16[384,512]{1,0:T(8,128)(2,1)} copy(bf16[384,512]{0,1:T(8,128)(2,1)} %bitcast.102) | data formatting | bytes 786432
  160.1 1.8 copy.158
  161.9 13.0 %reduce-scatter.3.cloned.1.call-done = bf16[128,1024]{0,1:T(8,128)(2,1)} async-done(((bf16[128,4096]{0,1:T(8,128)(2,1)}), bf16[128,1024]{0,1:T(8,128)(2,1)}) %reduce-scatter.3.cloned.1.call-update) | async-done | bytes 262160 | tf_op jit(solution)/shard_map/reduce_scatter | solution.py:172
  175.0 1.8 copy.157
  (83 shorter events, 19.2 us)
Async XLA Ops:
  7.2 110.6 %all-gather.5.cloned.1.call-start = ((), (), s32[]{:S(2)}) async-start(), calls=%async_computation.7 | async-start | bytes 1966080 | tf_op jit(solution)/shard_map/all_gather | solution.py:37
  7.9 8.7 %copy-start.16 = (bf16[384,512]{1,0:T(8,128)(2,1)S(1)}, bf16[384,512]{1,0:T(8,128)(2,1)}, u32[]{:S(2)}) copy-start(bf16[384,512]{1,0:T(8,128)(2,1)} %param.9) | copy-start | bytes 1179652
  9.6 8.0 %copy-start.17 = (s32[3,4]{1,0:T(4,128)S(1)}, s32[3,4]{1,0:T(4,128)}, u32[]{:S(2)}) copy-start(s32[3,4]{1,0:T(4,128)} %param.15) | copy-start | bytes 148
  9.6 8.7 %copy-start.8 = (bf16[384,512]{1,0:T(8,128)(2,1)S(1)}, bf16[384,512]{1,0:T(8,128)(2,1)}, u32[]{:S(2)}) copy-start(bf16[384,512]{1,0:T(8,128)(2,1)} %param.8) | copy-start | bytes 1179652
  9.6 8.8 %copy-start.11 = (bf16[384,512]{1,0:T(8,128)(2,1)S(1)}, bf16[384,512]{1,0:T(8,128)(2,1)}, u32[]{:S(2)}) copy-start(bf16[384,512]{1,0:T(8,128)(2,1)} %param.11) | copy-start | bytes 1179652
  11.0 8.6 %copy-start.13 = (bf16[128,4096]{1,0:T(8,128)(2,1)S(1)}, bf16[128,4096]{1,0:T(8,128)(2,1)}, u32[]{:S(2)}) copy-start(bf16[128,4096]{1,0:T(8,128)(2,1)} %param.13) | copy-start | bytes 3145732
  11.0 31.4 %all-to-all-start.1 = ((bf16[128,8,512]{2,0,1:T(8,128)(2,1)}), bf16[128,8,512]{2,0,1:T(8,128)(2,1)S(1)}, u32[]{:S(2)}, u32[]{:S(2)}) async-start(bf16[128,8,512]{2,0,1:T(8,128)(2,1)} %copy.123), calls=%async_computation.1 | async-start | bytes 2097152 | tf_op jit(solution)/shard_map/all_to_all | solution.py:53
  16.6 103.7 %all-gather.3.cloned.1.call-start = ((), (), s32[]{:S(2)}) async-start(), calls=%async_computation.6 | async-start | bytes 1966080 | tf_op jit(solution)/shard_map/all_gather | solution.py:36
  19.5 27.8 %copy-start.19 = (f32[4]{0:T(128)S(1)}, f32[4]{0:T(128)}, u32[]{:S(2)}) copy-start(f32[4]{0:T(128)} %param.14) | copy-start | bytes 52
  42.4 30.8 %all-to-all-start = ((bf16[128,8,512]{2,0,1:T(8,128)(2,1)}), bf16[128,8,512]{2,0,1:T(8,128)(2,1)}, u32[]{:S(2)}, u32[]{:S(2)}) async-start(bf16[128,8,512]{2,0,1:T(8,128)(2,1)} %copy.121), calls=%async_computation | async-start | bytes 2097152 | tf_op jit(solution)/shard_map/all_to_all | solution.py:54
  49.0 3.3 %copy-start.1 = (bf16[3,512,4,128]{3,2,1,0:T(4,128)(2,1)}, bf16[3,512,4,128]{3,2,1,0:T(4,128)(2,1)S(1)}, u32[]{:S(2)}) copy-start(bf16[3,512,4,128]{3,2,1,0:T(4,128)(2,1)S(1)} %reshape.112) | copy-start | bytes 4718596
  49.6 2.7 %copy-start.3 = (f32[3,4,512,128]{3,2,1,0:T(8,128)}, f32[3,4,512,128]{3,2,1,0:T(8,128)S(1)}, u32[]{:S(2)}) copy-start(f32[3,4,512,128]{3,2,1,0:T(8,128)S(1)} %fusion.29) | copy-start | bytes 9437188
  67.1 12.3 %copy-start.12 = (bf16[384,512]{1,0:T(8,128)(2,1)S(1)}, bf16[384,512]{1,0:T(8,128)(2,1)}, u32[]{:S(2)}) copy-start(bf16[384,512]{1,0:T(8,128)(2,1)} %param.11) | copy-start | bytes 1179652
  73.2 33.4 %all-to-all-start.3 = ((bf16[8,128,512]{2,1,0:T(8,128)(2,1)}), bf16[8,128,512]{2,1,0:T(8,128)(2,1)}, u32[]{:S(2)}, u32[]{:S(2)}) async-start(bf16[8,128,512]{2,1,0:T(8,128)(2,1)} %copy.153), calls=%async_computation.4 | async-start | bytes 2097152 | tf_op jit(solution)/shard_map/all_to_all | solution.py:169
  80.5 3.8 %copy-start.21 = (f32[4]{0:T(128)S(1)}, f32[4]{0:T(128)}, u32[]{:S(2)}) copy-start(f32[4]{0:T(128)} %get-tuple-element.25) | copy-start | bytes 52
  84.2 6.7 %copy-start.7 = (f32[3,4,128,512]{2,3,1,0:T(8,128)S(1)}, f32[3,4,128,512]{2,3,1,0:T(8,128)}, u32[]{:S(2)}) copy-start(f32[3,4,128,512]{2,3,1,0:T(8,128)} %get-tuple-element.31) | copy-start | bytes 9437188
  93.3 1.2 copy-start.4
  98.7 3.3 %copy-start.18 = (s32[12]{0:T(128)S(1)}, s32[12]{0:T(128)}, u32[]{:S(2)}) copy-start(s32[12]{0:T(128)} %eq.15) | copy-start | bytes 148
  106.6 8.0 %copy-start.2 = (bf16[3,512,4,128]{3,2,1,0:T(4,128)(2,1)S(1)}, bf16[3,512,4,128]{3,2,1,0:T(4,128)(2,1)}, u32[]{:S(2)}) copy-start(bf16[3,512,4,128]{3,2,1,0:T(4,128)(2,1)} %copy-done.1) | copy-start | bytes 4718596
  106.6 8.0 %copy-start.5 = (bf16[3,4,128,512]{2,3,1,0:T(8,128)(2,1)S(1)}, bf16[3,4,128,512]{2,3,1,0:T(8,128)(2,1)}, u32[]{:S(2)}) copy-start(bf16[3,4,128,512]{2,3,1,0:T(8,128)(2,1)} %copy-done.4) | copy-start | bytes 4718596
  106.6 31.2 %all-to-all-start.2 = ((bf16[8,128,512]{2,1,0:T(8,128)(2,1)}), bf16[8,128,512]{2,1,0:T(8,128)(2,1)}, u32[]{:S(2)}, u32[]{:S(2)}) async-start(bf16[8,128,512]{2,1,0:T(8,128)(2,1)} %copy.147), calls=%async_computation.2 | async-start | bytes 2097152 | tf_op jit(solution)/shard_map/all_to_all | solution.py:168
  112.0 48.1 %reduce-scatter.5.cloned.1.call-start = ((), (), s32[]{:S(2)}) async-start(), calls=%async_computation.9 | async-start | bytes 1310720 | tf_op jit(solution)/shard_map/reduce_scatter | solution.py:178
  114.3 60.7 %reduce-scatter.3.cloned.1.call-start = ((), (), s32[]{:S(2)}) async-start(), calls=%async_computation.8 | async-start | bytes 1310720 | tf_op jit(solution)/shard_map/reduce_scatter | solution.py:172
  115.3 1.2 copy-start.15
  116.5 3.8 %copy-start.6 = (pred[384,1536]{1,0:T(8,128)(4,1)S(1)}, pred[384,1536]{1,0:T(8,128)(4,1)}, u32[]{:S(2)}) copy-start(pred[384,1536]{1,0:T(8,128)(4,1)} %iota_compare_fusion) | copy-start | bytes 1769476
  116.6 3.8 %copy-start.9 = (bf16[384,512]{1,0:T(8,128)(2,1)S(1)}, bf16[384,512]{1,0:T(8,128)(2,1)}, u32[]{:S(2)}) copy-start(bf16[384,512]{1,0:T(8,128)(2,1)} %param.8) | copy-start | bytes 1179652
  123.8 3.7 %copy-start = (f32[4,384,1536]{2,1,0:T(8,128)}, f32[4,384,1536]{2,1,0:T(8,128)S(1)}, u32[]{:S(2)}) copy-start(f32[4,384,1536]{2,1,0:T(8,128)S(1)} %get-tuple-element.29) | copy-start | bytes 28311556
  127.4 12.7 %copy-start.14 = (f32[384,512]{0,1:T(8,128)S(1)}, f32[384,512]{0,1:T(8,128)}, u32[]{:S(2)}) copy-start(f32[384,512]{0,1:T(8,128)} %copy.140) | copy-start | bytes 2359300
  127.4 12.7 %copy-start.20 = (f32[4]{0:T(128)S(1)}, f32[4]{0:T(128)}, u32[]{:S(2)}) copy-start(f32[4]{0:T(128)} %get-tuple-element.24) | copy-start | bytes 52
  140.2 7.5 %copy-start.10 = (bf16[1536,512]{0,1:T(8,128)(2,1)S(1)}, bf16[1536,512]{0,1:T(8,128)(2,1)}, u32[]{:S(2)}) copy-start(bf16[1536,512]{0,1:T(8,128)(2,1)} %all-gather.3.cloned.1.call-done) | copy-start | bytes 4718596
Sparse Core Ops, SparseCore 0:
  9.8 32.1 all-gather.4
  44.5 30.7 all-gather.2
  115.7 28.4 reduce-scatter.4
  147.2 27.7 reduce-scatter.2
where the time goes:
time: 186 us; the launch traced here: 183 us
  waiting for transfers between devices  49.8 us (27%)
  local copies, waits for them, and re-layouts  47.1 us (25%)
  matrix products  43.3 us (23%)
  starting transfers between devices  21.3 us (11%)
  between operations  14.1 us (8%)
  other arithmetic  7.59 us (4%)
    all_to_all x1, waiting for transfers between devices, shards(): lax.all_to_all(mem_keys, 'mem', split_axis=1, concat_axis=0, tiled=True)  20.9 us
    reduce_scatter x1, waiting for transfers between devices, shards(): lax.psum_scatter(owner_keys.astype(jnp.float32).astype(jnp.bfloat16), 'ct...  13 us
    unnamed x51, local copies, waits for them, and re-layouts  11.4 us
    all_to_all x1, waiting for transfers between devices, shards(): lax.all_to_all(keys_low, 'mem', split_axis=0, concat_axis=1, tiled=True)  10.4 us
    dot_general x1, matrix products, shards(): jnp.einsum('hqk,khd->qhd', grad_scores.astype(jnp.bfloat16), shard_keys.r...  9.61 us
    dot_general x1, matrix products, shards(): jnp.einsum('hqk,khd->hqd', weights.astype(jnp.bfloat16), shard_values.res...  7.47 us
    dot_general x1, matrix products, shards(): jnp.einsum('bhqk,bkhd->bqhd', weights_reduced, selected_values, preferred...  6.7 us
    all_to_all x1, starting transfers between devices, shards(): lax.all_to_all(mem_keys, 'mem', split_axis=1, concat_axis=0, tiled=True)  5.68 us
  transfers between devices with their start and end apart: 8, of which 4 were waited for; matrix products, arithmetic and copies ran while one was open for 52% of the time, Pallas kernels for 0%

commit v1 on v0

v1 whole, which is shorter than its diff:
```python
import functools
import math

import jax
import jax.numpy as jnp
from jax import lax
from jax.experimental import pallas as pl
from jax.experimental.pallas import tpu as pltpu
from jax.sharding import PartitionSpec as P

HEAD_SIZE = 128
BLOCK = 128
MESH = pl.DeviceIdType.MESH
NEG = -1e30
F32 = jnp.float32
BF16 = jnp.bfloat16


def dot_nt(a, b):
    return lax.dot_general(a, b, (((1,), (1,)), ((), ())), preferred_element_type=F32)


def dot_nn(a, b):
    return lax.dot_general(a, b, (((1,), (0,)), ((), ())), preferred_element_type=F32)


def dot_tn(a, b):
    return lax.dot_general(a, b, (((0,), (0,)), ((), ())), preferred_element_type=F32)


def loop(low, high, body):
    def step(i, carry):
        body(i)
        return carry

    lax.fori_loop(low, high, step, 0)


def kernel(n_ctx, n_mem, ids, gate, q_ref, k_ref, v_ref, do_ref, mk_ref, mv_ref,
           mixed_ref, qg_ref, gk_ref, gv_ref,
           kall, vall, fk, fv, parts, recv, red, out, s_loc, s_mem,
           own_sem, fsend, frecv, lsend, lrecv, psend, precv, osend, orecv):
    c = lax.axis_index("ctx")
    m = lax.axis_index("mem")
    tok, width = q_ref.shape
    heads = width // HEAD_SIZE
    nqb = tok // BLOCK
    n_list = ids.shape[1]
    per = n_mem // n_ctx
    nsub = n_ctx // 2
    rs = BLOCK // nsub
    group = m // per
    col0 = lax.rem(m, per) * width
    scale = HEAD_SIZE ** -0.5
    scale2 = scale * math.log2(math.e)
    chunk = 2 * BLOCK
    n_chunk = n_mem * BLOCK // chunk

    def head(h, base=0):
        return pl.ds(pl.multiple_of(base + h * HEAD_SIZE, HEAD_SIZE), HEAD_SIZE)

    def rows(start, size):
        return pl.ds(pl.multiple_of(start, size), size)

    barrier = pltpu.get_barrier_semaphore()

    def greet(ctx, mem):
        pl.semaphore_signal(barrier, inc=1, device_id={"ctx": ctx, "mem": mem}, device_id_type=MESH)

    loop(1, n_mem, lambda d: greet(c, lax.rem(m + d, n_mem)))
    loop(1, n_ctx, lambda d: greet(lax.rem(c + d, n_ctx), m))

    def greet_owner(t):
        src_c, src_m = t // per, c * per + lax.rem(t, per)

        @pl.when(jnp.logical_or(src_c != c, src_m != m))
        def _():
            greet(src_c, src_m)

    loop(0, n_ctx * per, greet_owner)
    own_k = pltpu.make_async_copy(mk_ref.at[:, rows(m * width, width)], fk.at[rows(m * BLOCK, BLOCK)], own_sem.at[0])
    own_v = pltpu.make_async_copy(mv_ref.at[:, rows(m * width, width)], fv.at[rows(m * BLOCK, BLOCK)], own_sem.at[1])
    own_k.start()
    own_v.start()
    kall[c] = k_ref[...]
    vall[c] = v_ref[...]
    pl.semaphore_wait(barrier, n_mem - 1 + n_ctx - 1 + n_mem - jnp.where(group == c, 1, 0))

    def fetch(which, h, p):
        src, dst = ((mk_ref, fk), (mv_ref, fv))[which]
        return pltpu.make_async_remote_copy(
            src_ref=src.at[:, head(h, p * width)], dst_ref=dst.at[rows(m * BLOCK, BLOCK), head(h)],
            send_sem=fsend.at[which, h, p], recv_sem=frecv.at[which, h, m],
            device_id={"ctx": c, "mem": p}, device_id_type=MESH)

    def fetched(which, h, p):
        src, dst = ((mk_ref, fk), (mv_ref, fv))[which]
        return pltpu.make_async_remote_copy(
            src_ref=src.at[:, head(h, p * width)], dst_ref=dst.at[rows(p * BLOCK, BLOCK), head(h)],
            send_sem=fsend.at[which, h, p], recv_sem=frecv.at[which, h, p],
            device_id={"ctx": c, "mem": p}, device_id_type=MESH)

    def share(which, h, p, slot):
        src, dst = ((k_ref, kall), (v_ref, vall))[which]
        return pltpu.make_async_remote_copy(
            src_ref=src.at[:, head(h)], dst_ref=dst.at[slot, :, head(h)],
            send_sem=lsend.at[which, h, p], recv_sem=lrecv.at[which, h, slot],
            device_id={"ctx": p, "mem": m}, device_id_type=MESH)

    def part(h, p, slot):
        return pltpu.make_async_remote_copy(
            src_ref=parts.at[p, :, :, head(h)], dst_ref=recv.at[slot, :, :, head(h)],
            send_sem=psend.at[h, p], recv_sem=precv.at[h, slot],
            device_id={"ctx": p, "mem": m}, device_id_type=MESH)

    def owner_copy(h, r, src_c, src_i, base):
        return pltpu.make_async_remote_copy(
            src_ref=red.at[r, :, head(h)],
            dst_ref=out.at[src_c // nsub, rows(lax.rem(src_c, nsub) * rs, rs), head(h, base)],
            send_sem=osend.at[h, r], recv_sem=orecv.at[h, src_c, src_i],
            device_id={"ctx": group, "mem": r}, device_id_type=MESH)

    def start_head(h):
        def to_mem(d):
            p = lax.rem(m + d, n_mem)
            fetch(0, h, p).start()
            fetch(1, h, p).start()

        def to_ctx(p):
            share(0, h, p, c).start()
            share(1, h, p, c).start()

        loop(c + 1, n_ctx, to_ctx)
        loop(1, n_mem, to_mem)

    loop(0, heads, start_head)
    own_k.wait()
    own_v.wait()

    difference = (lax.broadcasted_iota(jnp.int32, (tok, tok), 1)
                  - lax.broadcasted_iota(jnp.int32, (tok, tok), 0))

    def listed(b, r):
        hit = ids[b, 0] == r
        for j in range(1, n_list):
            hit = jnp.logical_or(hit, ids[b, j] == r)
        return jnp.where(hit, 0.0, NEG).astype(F32)

    def reduce_head(h):
        total = parts[c, :, :, head(h)].astype(F32)

        def add(d, total):
            src = lax.rem(c + d, n_ctx)
            part(h, src, src).wait_recv()
            return total + recv[src, :, :, head(h)].astype(F32)

        total = lax.fori_loop(1, n_ctx, add, total)
        red[:, :, head(h)] = total.astype(BF16)

        def send(d):
            r = lax.rem(m + d, n_mem)
            owner_copy(h, r, c, lax.rem(m, per), col0).start()

        loop(1, n_mem, send)

        @pl.when(group == c)
        def _():
            out[c // nsub, rows(lax.rem(c, nsub) * rs, rs), head(h, col0)] = red[m, :, head(h)]

        @pl.when(group != c)
        def _():
            owner_copy(h, m, c, lax.rem(m, per), col0).start()

    def one_head(h):
        hc = head(h)
        q = q_ref[:, hc]
        g = 1.0 / (1.0 + jnp.exp(-jnp.full((1, HEAD_SIZE), gate[h], F32)))
        grad = do_ref[:, hc].astype(F32)
        dl = (1.0 - g) * grad
        dl_low = dl.astype(BF16)

        def wait_local(j):
            share(0, h, j, j).wait_recv()
            share(1, h, j, j).wait_recv()

        loop(0, c, wait_local)

        def scores(j, top):
            s = dot_nt(q, kall[j, :, hc]) * scale2
            s = jnp.where(difference <= (c - j) * tok, s, NEG)
            s_loc[j] = s
            return jnp.maximum(top, jnp.max(s, axis=-1, keepdims=True))

        top = lax.fori_loop(0, c + 1, scores, jnp.full((tok, 1), NEG, F32))

        def gather(j, carry):
            total, acc = carry
            e = jnp.exp2(s_loc[j] - top)
            s_loc[j] = e
            return (total + jnp.sum(e, axis=-1, keepdims=True),
                    acc + dot_nn(e.astype(BF16), vall[j, :, hc]))

        total, acc = lax.fori_loop(0, c + 1, gather, (jnp.zeros((tok, 1), F32), jnp.zeros((tok, HEAD_SIZE), F32)))
        inv = 1.0 / total
        local_out = acc * inv
        delta = jnp.sum(dl * local_out, axis=-1, keepdims=True)

        def back(j, acc):
            dp = dot_nt(dl_low, vall[j, :, hc])
            ds = (s_loc[j] * inv) * (dp - delta)
            return acc + dot_nn(ds.astype(BF16), kall[j, :, hc])

        local_grad = lax.fori_loop(0, c + 1, back, jnp.zeros((tok, HEAD_SIZE), F32))

        def wait_memory(d):
            p = lax.rem(m + d, n_mem)
            fetched(0, h, p).wait_recv()
            fetched(1, h, p).wait_recv()

        loop(1, n_mem, wait_memory)
        dm = g * grad
        dm_low = dm.astype(BF16)

        def mem_scores(i, top):
            s = dot_nt(q, fk[rows(i * chunk, chunk), hc]) * scale2
            bias = jnp.concatenate(
                [jnp.concatenate([jnp.full((BLOCK, BLOCK), listed(b, 2 * i + x), F32) for x in range(2)], axis=1)
                 for b in range(nqb)], axis=0)
            s = s + bias
            s_mem[i] = s
            return jnp.maximum(top, jnp.max(s, axis=-1, keepdims=True))

        top2 = lax.fori_loop(0, n_chunk, mem_scores, jnp.full((tok, 1), NEG, F32))

        def mem_gather(i, carry):
            total, acc = carry
            e = jnp.exp2(s_mem[i] - top2)
            s_mem[i] = e
            return (total + jnp.sum(e, axis=-1, keepdims=True),
                    acc + dot_nn(e.astype(BF16), fv[rows(i * chunk, chunk), hc]))

        total2, acc2 = lax.fori_loop(0, n_chunk, mem_gather,
                                     (jnp.zeros((tok, 1), F32), jnp.zeros((tok, HEAD_SIZE), F32)))
        inv2 = 1.0 / total2
        mem_out = acc2 * inv2
        mixed_ref[:, hc] = (g * mem_out + (1.0 - g) * local_out).astype(BF16)
        delta2 = jnp.sum(dm * mem_out, axis=-1, keepdims=True)

        def mem_back(i, acc):
            dw = dot_nt(dm_low, fv[rows(i * chunk, chunk), hc])
            w = s_mem[i] * inv2
            ds = (w * (dw - delta2)).astype(BF16)
            part_k = (dot_tn(ds, q) * scale).astype(BF16)
            part_v = dot_tn(w.astype(BF16), dm_low).astype(BF16)
            for x in range(2):
                for s in range(nsub):
                    at = slice(x * BLOCK + s * rs, x * BLOCK + (s + 1) * rs)
                    parts[s, 2 * i + x, :, hc] = part_k[at]
                    parts[nsub + s, 2 * i + x, :, hc] = part_v[at]
            return acc + dot_nn(ds, fk[rows(i * chunk, chunk), hc])

        mem_grad = lax.fori_loop(0, n_chunk, mem_back, jnp.zeros((tok, HEAD_SIZE), F32))
        qg_ref[:, hc] = ((local_grad + mem_grad) * scale).astype(BF16)

        loop(1, n_ctx, lambda d: part(h, lax.rem(c + d, n_ctx), c).start())

        @pl.when(h > 0)
        def _():
            reduce_head(h - 1)

    loop(0, heads, one_head)
    reduce_head(heads - 1)

    def finish(h):
        def arrived(t):
            src_c, i = t // per, lax.rem(t, per)

            @pl.when(jnp.logical_or(src_c != c, c * per + i != m))
            def _():
                owner_copy(h, m, src_c, i, i * width).wait_recv()

        def sent_mem(d):
            p = lax.rem(m + d, n_mem)
            fetch(0, h, p).wait_send()
            fetch(1, h, p).wait_send()
            owner_copy(h, p, c, lax.rem(m, per), col0).wait_send()

        def sent_ctx(p):
            share(0, h, p, c).wait_send()
            share(1, h, p, c).wait_send()

        loop(0, n_ctx * per, arrived)
        loop(1, n_mem, sent_mem)
        loop(c + 1, n_ctx, sent_ctx)
        loop(1, n_ctx, lambda d: part(h, lax.rem(c + d, n_ctx), c).wait_send())

        @pl.when(group != c)
        def _():
            owner_copy(h, m, c, lax.rem(m, per), col0).wait_send()

    loop(0, heads, finish)
    gk_ref[...] = out[0]
    gv_ref[...] = out[1]


def shards(n_ctx, n_mem, queries, keys, values, out_grad, mem_keys, mem_values, gate_logit, block_ids):
    tok, width = queries.shape
    columns = mem_keys.shape[1]
    heads = width // HEAD_SIZE
    rs = 2 * BLOCK // n_ctx
    mem_rows = n_mem * BLOCK
    vmem = pl.BlockSpec(memory_space=pltpu.VMEM)
    smem = pl.BlockSpec(memory_space=pltpu.SMEM)
    hbm = pl.BlockSpec(memory_space=pl.ANY)
    dma = pltpu.SemaphoreType.DMA
    pairs = (n_ctx + 1) * tok * tok * heads * HEAD_SIZE
    return pl.pallas_call(
        functools.partial(kernel, n_ctx, n_mem),
        out_shape=(
            jax.ShapeDtypeStruct((tok, width), BF16),
            jax.ShapeDtypeStruct((tok, width), BF16),
            jax.ShapeDtypeStruct((BLOCK, columns // n_ctx), BF16),
            jax.ShapeDtypeStruct((BLOCK, columns // n_ctx), BF16),
        ),
        in_specs=[smem, smem, vmem, vmem, vmem, vmem, hbm, hbm],
        out_specs=(vmem, vmem, vmem, vmem),
        scratch_shapes=[
            pltpu.VMEM((n_ctx, tok, width), BF16),
            pltpu.VMEM((n_ctx, tok, width), BF16),
            pltpu.VMEM((mem_rows, width), BF16),
            pltpu.VMEM((mem_rows, width), BF16),
            pltpu.VMEM((n_ctx, n_mem, rs, width), BF16),
            pltpu.VMEM((n_ctx, n_mem, rs, width), BF16),
            pltpu.VMEM((n_mem, rs, width), BF16),
            pltpu.VMEM((2, BLOCK, columns // n_ctx), BF16),
            pltpu.VMEM((n_ctx, tok, tok), F32),
            pltpu.VMEM((mem_rows // (2 * BLOCK), tok, 2 * BLOCK), F32),
            dma((2,)),
            dma((2, heads, n_mem)), dma((2, heads, n_mem)),
            dma((2, heads, n_ctx)), dma((2, heads, n_ctx)),
            dma((heads, n_ctx)), dma((heads, n_ctx)),
            dma((heads, n_mem)), dma((heads, n_ctx, n_mem // n_ctx)),
        ],
        compiler_params=pltpu.CompilerParams(
            collective_id=0, has_side_effects=True, vmem_limit_bytes=48 * 1024 * 1024
        ),
        cost_estimate=pl.CostEstimate(
            flops=8 * pairs, bytes_accessed=8 * 1024 * 1024, transcendentals=4 * tok * tok * heads
        ),
    )(block_ids, gate_logit, queries, keys, values, out_grad, mem_keys, mem_values)


def solution(mesh):
    in_specs = (
        P("ctx", "mem"),
        P("ctx", "mem"),
        P("ctx", "mem"),
        P("ctx", "mem"),
        P("mem", None),
        P("mem", None),
        P("mem"),
        P("ctx", None),
    )
    out_specs = (P("ctx", "mem"), P("ctx", "mem"), P("mem", "ctx"), P("mem", "ctx"))
    body = functools.partial(shards, mesh.shape["ctx"], mesh.shape["mem"])
    return jax.shard_map(body, mesh=mesh, in_specs=in_specs, out_specs=out_specs, check_vma=False)
```

time: 186 us -> 94.7 us (0.51); the launches traced: 183 us -> 93.9 us
  Pallas kernels: 0 us -> 82.6 us
  waiting for transfers between devices: 49.8 us -> 0 us
  matrix products: 43.3 us -> 0 us
  local copies, waits for them, and re-layouts: 47.1 us -> 10.7 us
  starting transfers between devices: 21.3 us -> 0 us
  between operations: 14.1 us -> 0.66 us
  other arithmetic: 7.59 us -> 0 us
    pallas_call x0 -> x1, Pallas kernels: none -> 82.6 us  [shards(): pl.pallas_call(functools.partial(kernel, n_ctx, n_mem), out_shape=(jax.Sh...]
    dot_general x11 -> x0, matrix products: 43.3 us -> none  [the longest x1 9.61 us: shards(): jnp.einsum('hqk,khd->qhd', grad_scores.astype(jnp.bfloat16), shard_keys.r...]
    all_to_all x4 -> x0, waiting for transfers between devices: 36.1 us -> none  [the longest x1 20.9 us: shards(): lax.all_to_all(mem_keys, 'mem', split_axis=1, concat_axis=0, tiled=True)]
    all_to_all x4 -> x0, starting transfers between devices: 21 us -> none  [the longest x1 5.68 us: shards(): lax.all_to_all(mem_keys, 'mem', split_axis=1, concat_axis=0, tiled=True)]
    reduce_scatter x2 -> x0, waiting for transfers between devices: 13 us -> none  [the longest x1 13 us: shards(): lax.psum_scatter(owner_keys.astype(jnp.float32).astype(jnp.bfloat16), 'ct...]
    reshape x7 -> x0, local copies, waits for them, and re-layouts: 11.3 us -> none  [the longest x1 3.32 us: shards(): selected_key_gradient.reshape(query_block_list * list_len, BLOCK, columns)]
    all_to_all x4 -> x0, local copies, waits for them, and re-layouts: 7.19 us -> none  [the longest x1 2.27 us: shards(): lax.all_to_all(keys_low, 'mem', split_axis=0, concat_axis=1, tiled=True)]
    convert_element_type x4 -> x0, local copies, waits for them, and re-layouts: 4.77 us -> none  [the longest x2 2.2 us: shards(): out_grad.reshape(tok_count, head_count, HEAD_SIZE).astype(jnp.float32)]
  transfers between devices with their start and end apart: 8 -> 0, of which waited for: 4 -> 0; matrix products, arithmetic and copies ran while one was open for 52% -> 0% of each run, Pallas kernels for 0% -> 0%
where the time goes in v1:
time: 94.7 us; the launch traced here: 93.9 us
  Pallas kernels  82.6 us (87%)
  local copies, waits for them, and re-layouts  10.7 us (11%)
    pallas_call x1, Pallas kernels, shards(): pl.pallas_call(functools.partial(kernel, n_ctx, n_mem), out_shape=(jax.Sh...  82.6 us
    unnamed x20, local copies, waits for them, and re-layouts  10.7 us

profile of v1, /device:TPU:3, one launch (start us, length us, event | category | flops | bytes accessed | tf_op | source)
XLA Modules:
  0.0 93.9 jit_solution(3925495467833563840)
XLA Ops:
  0.6 0.0 copy-start
  0.6 1.2 %copy-done = bf16[128,4096]{1,0:T(8,128)(2,1)S(1)} copy-done((bf16[128,4096]{1,0:T(8,128)(2,1)S(1)}, bf16[128,4096]{1,0:T(8,128)(2,1)}, u32[]{:S(2)}) %copy-start) | copy-done | bytes 1048600
  1.9 0.0 copy-start.1
  1.9 1.2 %copy-done.1 = bf16[128,4096]{1,0:T(8,128)(2,1)S(1)} copy-done((bf16[128,4096]{1,0:T(8,128)(2,1)S(1)}, bf16[128,4096]{1,0:T(8,128)(2,1)}, u32[]{:S(2)}) %copy-start.1) | copy-done | bytes 1048600
  3.1 0.0 copy-start.2
  3.1 1.0 %copy-done.2 = bf16[384,512]{1,0:T(8,128)(2,1)S(1)} copy-done((bf16[384,512]{1,0:T(8,128)(2,1)S(1)}, bf16[384,512]{1,0:T(8,128)(2,1)}, u32[]{:S(2)}) %copy-start.2) | copy-done | bytes 393240
  4.1 0.0 copy-start.3
  4.1 1.0 %copy-done.3 = bf16[384,512]{1,0:T(8,128)(2,1)S(1)} copy-done((bf16[384,512]{1,0:T(8,128)(2,1)S(1)}, bf16[384,512]{1,0:T(8,128)(2,1)}, u32[]{:S(2)}) %copy-start.3) | copy-done | bytes 393240
  5.1 0.0 copy-start.4
  5.1 1.0 %copy-done.4 = bf16[384,512]{1,0:T(8,128)(2,1)S(1)} copy-done((bf16[384,512]{1,0:T(8,128)(2,1)S(1)}, bf16[384,512]{1,0:T(8,128)(2,1)}, u32[]{:S(2)}) %copy-start.4) | copy-done | bytes 393240
  6.1 0.0 copy-start.5
  6.1 1.0 %copy-done.5 = bf16[384,512]{1,0:T(8,128)(2,1)S(1)} copy-done((bf16[384,512]{1,0:T(8,128)(2,1)S(1)}, bf16[384,512]{1,0:T(8,128)(2,1)}, u32[]{:S(2)}) %copy-start.5) | copy-done | bytes 393240
  7.1 0.0 copy-start.6
  7.1 0.7 copy-done.6
  7.8 0.0 copy-start.7
  7.8 0.7 copy-done.7
  8.4 82.6 %shard_map.111 = (bf16[384,512]{1,0:T(8,128)(2,1)S(1)}, bf16[384,512]{1,0:T(8,128)(2,1)S(1)}, bf16[128,1024]{1,0:T(8,128)(2,1)S(1)}, bf16[128,1024]{1,0:T(8,128)(2,1)S(1)}) custom-call(s32[3,4]{1,0:T(4,128)S(1)} %copy-done.6, f32[4]{0:T(128)S(1)} %copy-done.7, bf16[384,512]{1,0:T(8,128)(2,1)S(1)} %copy-done.2, bf16[384,512]{1,0:T(8,128)(2,1)S(1)} %copy-done.3, ...), custom_call_target="tpu_custom_call" | custom-call | flops 3019898880 | bytes 8388608 | tf_op jit(solution)/shard_map/pallas_call | solution.py:317
  91.0 0.7 copy.16
  91.8 0.7 copy.17
  92.5 0.7 copy.18
  93.2 0.7 copy.19
Async XLA Ops:
  0.6 1.2 %copy-start = (bf16[128,4096]{1,0:T(8,128)(2,1)S(1)}, bf16[128,4096]{1,0:T(8,128)(2,1)}, u32[]{:S(2)}) copy-start(bf16[128,4096]{1,0:T(8,128)(2,1)} %mk_ref.1) | copy-start | bytes 3145732
  1.9 1.2 %copy-start.1 = (bf16[128,4096]{1,0:T(8,128)(2,1)S(1)}, bf16[128,4096]{1,0:T(8,128)(2,1)}, u32[]{:S(2)}) copy-start(bf16[128,4096]{1,0:T(8,128)(2,1)} %mv_ref.1) | copy-start | bytes 3145732
  3.1 1.0 %copy-start.2 = (bf16[384,512]{1,0:T(8,128)(2,1)S(1)}, bf16[384,512]{1,0:T(8,128)(2,1)}, u32[]{:S(2)}) copy-start(bf16[384,512]{1,0:T(8,128)(2,1)} %q_ref.1) | copy-start | bytes 1179652
  4.1 1.0 %copy-start.3 = (bf16[384,512]{1,0:T(8,128)(2,1)S(1)}, bf16[384,512]{1,0:T(8,128)(2,1)}, u32[]{:S(2)}) copy-start(bf16[384,512]{1,0:T(8,128)(2,1)} %k_ref.1) | copy-start | bytes 1179652
  5.1 1.0 %copy-start.4 = (bf16[384,512]{1,0:T(8,128)(2,1)S(1)}, bf16[384,512]{1,0:T(8,128)(2,1)}, u32[]{:S(2)}) copy-start(bf16[384,512]{1,0:T(8,128)(2,1)} %v_ref.1) | copy-start | bytes 1179652
  6.1 1.0 %copy-start.5 = (bf16[384,512]{1,0:T(8,128)(2,1)S(1)}, bf16[384,512]{1,0:T(8,128)(2,1)}, u32[]{:S(2)}) copy-start(bf16[384,512]{1,0:T(8,128)(2,1)} %do_ref.1) | copy-start | bytes 1179652
  7.1 0.7 copy-start.6
  7.8 0.7 copy-start.7

commit v2 on v1

--- a/solution.py
+++ b/solution.py
@@ -36,13 +36,13 @@
     lax.fori_loop(low, high, step, 0)
 
 
-def kernel(n_ctx, n_mem, ids, gate, q_ref, k_ref, v_ref, do_ref, mk_ref, mv_ref,
+def kernel(n_ctx, n_mem, ids_in, gate_in, q_in, k_ref, v_ref, do_in, mk_ref, mv_ref,
            mixed_ref, qg_ref, gk_ref, gv_ref,
-           kall, vall, fk, fv, parts, recv, red, out, s_loc, s_mem,
+           ids, gate, q_ref, do_ref, l_out, l_grad, m_out, m_grad, kall, vall, fk, fv, parts, recv, red, out, s_loc, s_mem,
            own_sem, fsend, frecv, lsend, lrecv, psend, precv, osend, orecv):
     c = lax.axis_index("ctx")
     m = lax.axis_index("mem")
-    tok, width = q_ref.shape
+    tok, width = q_in.shape
     heads = width // HEAD_SIZE
     nqb = tok // BLOCK
     n_list = ids.shape[1]
@@ -80,10 +80,18 @@
     loop(0, n_ctx * per, greet_owner)
     own_k = pltpu.make_async_copy(mk_ref.at[:, rows(m * width, width)], fk.at[rows(m * BLOCK, BLOCK)], own_sem.at[0])
     own_v = pltpu.make_async_copy(mv_ref.at[:, rows(m * width, width)], fv.at[rows(m * BLOCK, BLOCK)], own_sem.at[1])
-    own_k.start()
-    own_v.start()
-    kall[c] = k_ref[...]
-    vall[c] = v_ref[...]
+    mine = [
+        pltpu.make_async_copy(ids_in, ids, own_sem.at[2]),
+        pltpu.make_async_copy(gate_in, gate, own_sem.at[3]),
+        pltpu.make_async_copy(q_in, q_ref, own_sem.at[4]),
+        pltpu.make_async_copy(do_in, do_ref, own_sem.at[5]),
+        pltpu.make_async_copy(k_ref, kall.at[c], own_sem.at[6]),
+        pltpu.make_async_copy(v_ref, vall.at[c], own_sem.at[7]),
+        own_k,
+        own_v,
+    ]
+    for copy in mine:
+        copy.start()
     pl.semaphore_wait(barrier, n_mem - 1 + n_ctx - 1 + n_mem - jnp.where(group == c, 1, 0))
 
     def fetch(which, h, p):
@@ -134,8 +142,8 @@
         loop(1, n_mem, to_mem)
 
     loop(0, heads, start_head)
-    own_k.wait()
-    own_v.wait()
+    for copy in mine:
+        copy.wait()
 
     difference = (lax.broadcasted_iota(jnp.int32, (tok, tok), 1)
                   - lax.broadcasted_iota(jnp.int32, (tok, tok), 0))
@@ -171,10 +179,13 @@
         def _():
             owner_copy(h, m, c, lax.rem(m, per), col0).start()
 
-    def one_head(h):
+    def share_of_gate(h):
+        return 1.0 / (1.0 + jnp.exp(-jnp.full((1, HEAD_SIZE), gate[h], F32)))
+
+    def local_head(h):
         hc = head(h)
         q = q_ref[:, hc]
-        g = 1.0 / (1.0 + jnp.exp(-jnp.full((1, HEAD_SIZE), gate[h], F32)))
+        g = share_of_gate(h)
         grad = do_ref[:, hc].astype(F32)
         dl = (1.0 - g) * grad
         dl_low = dl.astype(BF16)
@@ -210,7 +221,14 @@
             ds = (s_loc[j] * inv) * (dp - delta)
             return acc + dot_nn(ds.astype(BF16), kall[j, :, hc])
 
-        local_grad = lax.fori_loop(0, c + 1, back, jnp.zeros((tok, HEAD_SIZE), F32))
+        l_grad[:, hc] = lax.fori_loop(0, c + 1, back, jnp.zeros((tok, HEAD_SIZE), F32))
+        l_out[:, hc] = (1.0 - g) * local_out
+
+    def mem_head(h):
+        hc = head(h)
+        q = q_ref[:, hc]
+        g = share_of_gate(h)
+        grad = do_ref[:, hc].astype(F32)
 
         def wait_memory(d):
             p = lax.rem(m + d, n_mem)
@@ -243,7 +261,7 @@
                                      (jnp.zeros((tok, 1), F32), jnp.zeros((tok, HEAD_SIZE), F32)))
         inv2 = 1.0 / total2
         mem_out = acc2 * inv2
-        mixed_ref[:, hc] = (g * mem_out + (1.0 - g) * local_out).astype(BF16)
+        m_out[:, hc] = g * mem_out
         delta2 = jnp.sum(dm * mem_out, axis=-1, keepdims=True)
 
         def mem_back(i, acc):
@@ -259,17 +277,25 @@
                     parts[nsub + s, 2 * i + x, :, hc] = part_v[at]
             return acc + dot_nn(ds, fk[rows(i * chunk, chunk), hc])
 
-        mem_grad = lax.fori_loop(0, n_chunk, mem_back, jnp.zeros((tok, HEAD_SIZE), F32))
-        qg_ref[:, hc] = ((local_grad + mem_grad) * scale).astype(BF16)
-
+        m_grad[:, hc] = lax.fori_loop(0, n_chunk, mem_back, jnp.zeros((tok, HEAD_SIZE), F32))
         loop(1, n_ctx, lambda d: part(h, lax.rem(c + d, n_ctx), c).start())
 
+    def one_head(h):
+        @pl.when(h < heads - 1)
+        def _():
+            local_head(h)
+
+        mem_head(h)
+
         @pl.when(h > 0)
         def _():
             reduce_head(h - 1)
 
     loop(0, heads, one_head)
+    local_head(heads - 1)
     reduce_head(heads - 1)
+    mixed_ref[...] = (m_out[...] + l_out[...]).astype(BF16)
+    qg_ref[...] = ((m_grad[...] + l_grad[...]) * scale).astype(BF16)
 
     def finish(h):
         def arrived(t):
@@ -301,6 +327,17 @@
     loop(0, heads, finish)
     gk_ref[...] = out[0]
     gv_ref[...] = out[1]
+
+
+def hand_on(a, b, c, d, a_out, b_out, c_out, d_out, sem):
+    copies = [
+        pltpu.make_async_copy(src, dst, sem.at[i])
+        for i, (src, dst) in enumerate(((a, a_out), (b, b_out), (c, c_out), (d, d_out)))
+    ]
+    for copy in copies:
+        copy.start()
+    for copy in copies:
+        copy.wait()
 
 
 def shards(n_ctx, n_mem, queries, keys, values, out_grad, mem_keys, mem_values, gate_logit, block_ids):
@@ -310,11 +347,10 @@
     rs = 2 * BLOCK // n_ctx
     mem_rows = n_mem * BLOCK
     vmem = pl.BlockSpec(memory_space=pltpu.VMEM)
-    smem = pl.BlockSpec(memory_space=pltpu.SMEM)
     hbm = pl.BlockSpec(memory_space=pl.ANY)
     dma = pltpu.SemaphoreType.DMA
     pairs = (n_ctx + 1) * tok * tok * heads * HEAD_SIZE
-    return pl.pallas_call(
+    results = pl.pallas_call(
         functools.partial(kernel, n_ctx, n_mem),
         out_shape=(
             jax.ShapeDtypeStruct((tok, width), BF16),
@@ -322,9 +358,17 @@
             jax.ShapeDtypeStruct((BLOCK, columns // n_ctx), BF16),
             jax.ShapeDtypeStruct((BLOCK, columns // n_ctx), BF16),
         ),
-        in_specs=[smem, smem, vmem, vmem, vmem, vmem, hbm, hbm],
+        in_specs=[hbm] * 8,
         out_specs=(vmem, vmem, vmem, vmem),
         scratch_shapes=[
+            pltpu.SMEM(block_ids.shape, jnp.int32),
+            pltpu.SMEM(gate_logit.shape, F32),
+            pltpu.VMEM((tok, width), BF16),
+            pltpu.VMEM((tok, width), BF16),
+            pltpu.VMEM((tok, width), F32),
+            pltpu.VMEM((tok, width), F32),
+            pltpu.VMEM((tok, width), F32),
+            pltpu.VMEM((tok, width), F32),
             pltpu.VMEM((n_ctx, tok, width), BF16),
             pltpu.VMEM((n_ctx, tok, width), BF16),
             pltpu.VMEM((mem_rows, width), BF16),
@@ -335,19 +379,27 @@
             pltpu.VMEM((2, BLOCK, columns // n_ctx), BF16),
             pltpu.VMEM((n_ctx, tok, tok), F32),
             pltpu.VMEM((mem_rows // (2 * BLOCK), tok, 2 * BLOCK), F32),
-            dma((2,)),
+            dma((8,)),
             dma((2, heads, n_mem)), dma((2, heads, n_mem)),
             dma((2, heads, n_ctx)), dma((2, heads, n_ctx)),
             dma((heads, n_ctx)), dma((heads, n_ctx)),
             dma((heads, n_mem)), dma((heads, n_ctx, n_mem // n_ctx)),
         ],
         compiler_params=pltpu.CompilerParams(
-            collective_id=0, has_side_effects=True, vmem_limit_bytes=48 * 1024 * 1024
+            collective_id=0, has_side_effects=True, vmem_limit_bytes=62 * 1024 * 1024
         ),
         cost_estimate=pl.CostEstimate(
             flops=8 * pairs, bytes_accessed=8 * 1024 * 1024, transcendentals=4 * tok * tok * heads
         ),
     )(block_ids, gate_logit, queries, keys, values, out_grad, mem_keys, mem_values)
+    return pl.pallas_call(
+        hand_on,
+        out_shape=tuple(jax.ShapeDtypeStruct(r.shape, r.dtype) for r in results),
+        in_specs=[hbm] * 4,
+        out_specs=(hbm,) * 4,
+        scratch_shapes=[dma((4,))],
+        compiler_params=pltpu.CompilerParams(vmem_limit_bytes=62 * 1024 * 1024),
+    )(*results)
 
 
 def solution(mesh):

time: 94.7 us -> 123 us (1.30)
  Pallas kernels: 82.6 us -> 121 us
  local copies, waits for them, and re-layouts: 10.7 us -> 0 us
    pallas_call x0 -> x1, Pallas kernels: none -> 40.8 us  [shards(): pl.pallas_call(hand_on, out_shape=tuple((jax.ShapeDtypeStruct(r.shape, r....]
    unnamed x20 -> x0, local copies, waits for them, and re-layouts: 10.7 us -> none
    pallas_call x1, Pallas kernels: 82.6 us -> 80.6 us  [shards(): pl.pallas_call(functools.partial(kernel, n_ctx, n_mem), out_shape=(jax.Sh...]
where the time goes in v2:
time: 123 us; the launch traced here: 122 us
  Pallas kernels  121 us (98%)
    pallas_call x1, Pallas kernels, shards(): pl.pallas_call(functools.partial(kernel, n_ctx, n_mem), out_shape=(jax.Sh...  80.6 us
    pallas_call x1, Pallas kernels, shards(): pl.pallas_call(hand_on, out_shape=tuple((jax.ShapeDtypeStruct(r.shape, r....  40.8 us

profile of v2, /device:TPU:3, one launch (start us, length us, event | category | flops | bytes accessed | tf_op | source)
XLA Modules:
  0.0 122.1 jit_solution(8992370566846686414)
XLA Ops:
  0.6 80.6 %shard_map.111 = (bf16[384,512]{1,0:T(8,128)(2,1)}, bf16[384,512]{1,0:T(8,128)(2,1)}, bf16[128,1024]{1,0:T(8,128)(2,1)}, bf16[128,1024]{1,0:T(8,128)(2,1)}) custom-call(s32[3,4]{1,0:T(4,128)} %ids_in.1, f32[4]{0:T(128)} %gate_in.1, bf16[384,512]{1,0:T(8,128)(2,1)} %q_in.1, bf16[384,512]{1,0:T(8,128)(2,1)} %k_ref.1, bf16[384,512]{1,0:T(8,128)(2,1)} %v_ref.1, ...), custom_call_target="tpu_custom_call" | custom-call | flops 3019898880 | bytes 8388608 | tf_op jit(solution)/shard_map/pallas_call | solution.py:353
  81.2 40.8 %shard_map.112 = (bf16[384,512]{1,0:T(8,128)(2,1)}, bf16[384,512]{1,0:T(8,128)(2,1)}, bf16[128,1024]{1,0:T(8,128)(2,1)}, bf16[128,1024]{1,0:T(8,128)(2,1)}) custom-call(bf16[384,512]{1,0:T(8,128)(2,1)} %get-tuple-element.8.a, bf16[384,512]{1,0:T(8,128)(2,1)} %get-tuple-element.9.b, bf16[128,1024]{1,0:T(8,128)(2,1)} %get-tuple-element.10.c, ...), custom_call_target="tpu_custom_call" | custom-call | tf_op jit(solution)/shard_map/pallas_call | solution.py:395

commit v3 on v2

--- a/solution.py
+++ b/solution.py
@@ -11,6 +11,7 @@
 HEAD_SIZE = 128
 BLOCK = 128
 MESH = pl.DeviceIdType.MESH
+UNIT = 16
 NEG = -1e30
 F32 = jnp.float32
 BF16 = jnp.bfloat16
@@ -38,8 +39,8 @@
 
 def kernel(n_ctx, n_mem, ids_in, gate_in, q_in, k_ref, v_ref, do_in, mk_ref, mv_ref,
            mixed_ref, qg_ref, gk_ref, gv_ref,
-           ids, gate, q_ref, do_ref, l_out, l_grad, m_out, m_grad, kall, vall, fk, fv, parts, recv, red, out, s_loc, s_mem,
-           own_sem, fsend, frecv, lsend, lrecv, psend, precv, osend, orecv):
+           ids, gate, q_ref, do_ref, l_out, l_grad, m_out, m_grad, kall, vall, fkv, parts, recv, red, out, s_loc, s_mem,
+           own_sem, fsend, frecv, csend, crecv, rsend, rrecv, lsend, lrecv, wsend, psend, precv, osend, orecv):
     c = lax.axis_index("ctx")
     m = lax.axis_index("mem")
     tok, width = q_in.shape
@@ -55,6 +56,11 @@
     scale2 = scale * math.log2(math.e)
     chunk = 2 * BLOCK
     n_chunk = n_mem * BLOCK // chunk
+    unit = UNIT
+    direct = BLOCK - nsub * unit
+    mine_kv = c // nsub
+    mine_row = direct + lax.rem(c, nsub) * unit
+    four = n_ctx == 4
 
     def head(h, base=0):
         return pl.ds(pl.multiple_of(base + h * HEAD_SIZE, HEAD_SIZE), HEAD_SIZE)
@@ -78,8 +84,6 @@
             greet(src_c, src_m)
 
     loop(0, n_ctx * per, greet_owner)
-    own_k = pltpu.make_async_copy(mk_ref.at[:, rows(m * width, width)], fk.at[rows(m * BLOCK, BLOCK)], own_sem.at[0])
-    own_v = pltpu.make_async_copy(mv_ref.at[:, rows(m * width, width)], fv.at[rows(m * BLOCK, BLOCK)], own_sem.at[1])
     mine = [
         pltpu.make_async_copy(ids_in, ids, own_sem.at[2]),
         pltpu.make_async_copy(gate_in, gate, own_sem.at[3]),
@@ -87,26 +91,52 @@
         pltpu.make_async_copy(do_in, do_ref, own_sem.at[5]),
         pltpu.make_async_copy(k_ref, kall.at[c], own_sem.at[6]),
         pltpu.make_async_copy(v_ref, vall.at[c], own_sem.at[7]),
-        own_k,
-        own_v,
     ]
+    if direct:
+        mine += [
+            pltpu.make_async_copy(src.at[pl.ds(0, direct), rows(m * width, width)],
+                                  fkv.at[i, m, pl.ds(0, direct)], own_sem.at[i])
+            for i, src in enumerate((mk_ref, mv_ref))
+        ]
     for copy in mine:
         copy.start()
     pl.semaphore_wait(barrier, n_mem - 1 + n_ctx - 1 + n_mem - jnp.where(group == c, 1, 0))
 
-    def fetch(which, h, p):
-        src, dst = ((mk_ref, fk), (mv_ref, fv))[which]
-        return pltpu.make_async_remote_copy(
-            src_ref=src.at[:, head(h, p * width)], dst_ref=dst.at[rows(m * BLOCK, BLOCK), head(h)],
-            send_sem=fsend.at[which, h, p], recv_sem=frecv.at[which, h, m],
+    def fetch(which, h, p, slot):
+        return pltpu.make_async_remote_copy(
+            src_ref=(mk_ref, mv_ref)[which].at[pl.ds(0, direct), head(h, p * width)],
+            dst_ref=fkv.at[which, slot, pl.ds(0, direct), head(h)],
+            send_sem=fsend.at[which, h, p], recv_sem=frecv.at[which, h, slot],
             device_id={"ctx": c, "mem": p}, device_id_type=MESH)
 
-    def fetched(which, h, p):
-        src, dst = ((mk_ref, fk), (mv_ref, fv))[which]
-        return pltpu.make_async_remote_copy(
-            src_ref=src.at[:, head(h, p * width)], dst_ref=dst.at[rows(p * BLOCK, BLOCK), head(h)],
-            send_sem=fsend.at[which, h, p], recv_sem=frecv.at[which, h, p],
+    def piece(which, p, slot):
+        return pltpu.make_async_remote_copy(
+            src_ref=(mk_ref, mv_ref)[which].at[rows(mine_row, unit), rows(p * width, width)],
+            dst_ref=fkv.at[which, slot, rows(mine_row, unit)],
+            send_sem=csend.at[p], recv_sem=crecv.at[slot],
             device_id={"ctx": c, "mem": p}, device_id_type=MESH)
+
+    def own_piece(which):
+        return pltpu.make_async_copy(
+            (mk_ref, mv_ref)[which].at[rows(mine_row, unit), rows(m * width, width)],
+            fkv.at[which, m, rows(mine_row, unit)], own_sem.at[8])
+
+    def relay(p, src):
+        at = fkv.at[src // nsub, :, rows(direct + lax.rem(src, nsub) * unit, unit)]
+        return pltpu.make_async_remote_copy(
+            src_ref=at, dst_ref=at, send_sem=rsend.at[p], recv_sem=rrecv.at[src],
+            device_id={"ctx": p, "mem": m}, device_id_type=MESH)
+
+    def both(do):
+        for which in range(2):
+            pl.when(mine_kv == which)(functools.partial(do, which))
+
+    def forward(which, h, p, slot):
+        buf = (kall, vall)[which]
+        return pltpu.make_async_remote_copy(
+            src_ref=buf.at[slot, :, head(h)], dst_ref=buf.at[slot, :, head(h)],
+            send_sem=wsend.at[which, h], recv_sem=lrecv.at[which, h, slot],
+            device_id={"ctx": p, "mem": m}, device_id_type=MESH)
 
     def share(which, h, p, slot):
         src, dst = ((k_ref, kall), (v_ref, vall))[which]
@@ -128,22 +158,56 @@
             send_sem=osend.at[h, r], recv_sem=orecv.at[h, src_c, src_i],
             device_id={"ctx": group, "mem": r}, device_id_type=MESH)
 
-    def start_head(h):
+    def apart(p):
+        return c + p != 3 if four else p >= 0
+
+    def start_share(h):
+        def to_ctx(p):
+            @pl.when(apart(p))
+            def _():
+                share(0, h, p, c).start()
+                share(1, h, p, c).start()
+
+        loop(c + 1, n_ctx, to_ctx)
+
+    def start_fetch(h):
         def to_mem(d):
             p = lax.rem(m + d, n_mem)
-            fetch(0, h, p).start()
-            fetch(1, h, p).start()
-
-        def to_ctx(p):
-            share(0, h, p, c).start()
-            share(1, h, p, c).start()
-
-        loop(c + 1, n_ctx, to_ctx)
+            fetch(0, h, p, m).start()
+            fetch(1, h, p, m).start()
+
         loop(1, n_mem, to_mem)
 
-    loop(0, heads, start_head)
+    def send_pieces(which):
+        own_piece(which).start()
+        loop(1, n_mem, lambda d: piece(which, lax.rem(m + d, n_mem), m).start())
+
+    def take_pieces(which):
+        own_piece(which).wait()
+
+        def take(d):
+            p = lax.rem(m + d, n_mem)
+            piece(which, p, p).wait_recv()
+
+        loop(1, n_mem, take)
+
+    both(send_pieces)
+    start_share(0)
+    if direct:
+        loop(0, heads, start_fetch)
     for copy in mine:
         copy.wait()
+    both(take_pieces)
+    loop(1, n_ctx, lambda d: relay(lax.rem(c + d, n_ctx), c).start())
+    loop(1, heads, start_share)
+
+    def pass_on(h):
+        if four:
+            for at, which, slot, to in ((1, 0, 0, 3), (2, 1, 0, 3), (3, 0, 1, 2), (3, 1, 1, 2)):
+                @pl.when(c == at)
+                def _(which=which, slot=slot, to=to):
+                    share(which, h, slot, slot).wait_recv()
+                    forward(which, h, to, slot).start()
 
     difference = (lax.broadcasted_iota(jnp.int32, (tok, tok), 1)
                   - lax.broadcasted_iota(jnp.int32, (tok, tok), 0))
@@ -191,8 +255,12 @@
         dl_low = dl.astype(BF16)
 
         def wait_local(j):
-            share(0, h, j, j).wait_recv()
-            share(1, h, j, j).wait_recv()
+            for which in range(2):
+                if four:
+                    ahead = jnp.logical_or(jnp.logical_and(c == 1 + which, j == 0), jnp.logical_and(c == 3, j == 1))
+                    pl.when(jnp.logical_not(ahead))(lambda: share(which, h, j, j).wait_recv())
+                else:
+                    share(which, h, j, j).wait_recv()
 
         loop(0, c, wait_local)
 
@@ -232,15 +300,29 @@
 
         def wait_memory(d):
             p = lax.rem(m + d, n_mem)
-            fetched(0, h, p).wait_recv()
-            fetched(1, h, p).wait_recv()
-
-        loop(1, n_mem, wait_memory)
+            fetch(0, h, p, p).wait_recv()
+            fetch(1, h, p, p).wait_recv()
+
+        if direct:
+            loop(1, n_mem, wait_memory)
+
+        @pl.when(h == 0)
+        def _():
+            def wait_relay(d):
+                src = lax.rem(c + d, n_ctx)
+                relay(src, src).wait_recv()
+
+            loop(1, n_ctx, wait_relay)
+
+        def rows_of(which, i):
+            return jnp.concatenate([fkv[which, 2 * i + x, :, hc] for x in range(2)], axis=0)
+
+        unroll = math.gcd(n_chunk, 4)
         dm = g * grad
         dm_low = dm.astype(BF16)
 
         def mem_scores(i, top):
-            s = dot_nt(q, fk[rows(i * chunk, chunk), hc]) * scale2
+            s = dot_nt(q, rows_of(0, i)) * scale2
             bias = jnp.concatenate(
                 [jnp.concatenate([jnp.full((BLOCK, BLOCK), listed(b, 2 * i + x), F32) for x in range(2)], axis=1)
                  for b in range(nqb)], axis=0)
@@ -248,24 +330,24 @@
             s_mem[i] = s
             return jnp.maximum(top, jnp.max(s, axis=-1, keepdims=True))
 
-        top2 = lax.fori_loop(0, n_chunk, mem_scores, jnp.full((tok, 1), NEG, F32))
+        top2 = lax.fori_loop(0, n_chunk, mem_scores, jnp.full((tok, 1), NEG, F32), unroll=unroll)
 
         def mem_gather(i, carry):
             total, acc = carry
             e = jnp.exp2(s_mem[i] - top2)
             s_mem[i] = e
             return (total + jnp.sum(e, axis=-1, keepdims=True),
-                    acc + dot_nn(e.astype(BF16), fv[rows(i * chunk, chunk), hc]))
+                    acc + dot_nn(e.astype(BF16), rows_of(1, i)))
 
         total2, acc2 = lax.fori_loop(0, n_chunk, mem_gather,
-                                     (jnp.zeros((tok, 1), F32), jnp.zeros((tok, HEAD_SIZE), F32)))
+                                     (jnp.zeros((tok, 1), F32), jnp.zeros((tok, HEAD_SIZE), F32)), unroll=unroll)
         inv2 = 1.0 / total2
         mem_out = acc2 * inv2
         m_out[:, hc] = g * mem_out
         delta2 = jnp.sum(dm * mem_out, axis=-1, keepdims=True)
 
         def mem_back(i, acc):
-            dw = dot_nt(dm_low, fv[rows(i * chunk, chunk), hc])
+            dw = dot_nt(dm_low, rows_of(1, i))
             w = s_mem[i] * inv2
             ds = (w * (dw - delta2)).astype(BF16)
             part_k = (dot_tn(ds, q) * scale).astype(BF16)
@@ -275,9 +357,9 @@
                     at = slice(x * BLOCK + s * rs, x * BLOCK + (s + 1) * rs)
                     parts[s, 2 * i + x, :, hc] = part_k[at]
                     parts[nsub + s, 2 * i + x, :, hc] = part_v[at]
-            return acc + dot_nn(ds, fk[rows(i * chunk, chunk), hc])
-
-        m_grad[:, hc] = lax.fori_loop(0, n_chunk, mem_back, jnp.zeros((tok, HEAD_SIZE), F32))
+            return acc + dot_nn(ds, rows_of(0, i))
+
+        m_grad[:, hc] = lax.fori_loop(0, n_chunk, mem_back, jnp.zeros((tok, HEAD_SIZE), F32), unroll=unroll)
         loop(1, n_ctx, lambda d: part(h, lax.rem(c + d, n_ctx), c).start())
 
     def one_head(h):
@@ -285,12 +367,17 @@
         def _():
             local_head(h)
 
+        @pl.when(h < heads - 1)
+        def _():
+            pass_on(h + 1)
+
         mem_head(h)
 
         @pl.when(h > 0)
         def _():
             reduce_head(h - 1)
 
+    pass_on(0)
     loop(0, heads, one_head)
     local_head(heads - 1)
     reduce_head(heads - 1)
@@ -307,13 +394,20 @@
 
         def sent_mem(d):
             p = lax.rem(m + d, n_mem)
-            fetch(0, h, p).wait_send()
-            fetch(1, h, p).wait_send()
+            if direct:
+                fetch(0, h, p, m).wait_send()
+                fetch(1, h, p, m).wait_send()
             owner_copy(h, p, c, lax.rem(m, per), col0).wait_send()
 
         def sent_ctx(p):
-            share(0, h, p, c).wait_send()
-            share(1, h, p, c).wait_send()
+            @pl.when(apart(p))
+            def _():
+                share(0, h, p, c).wait_send()
+                share(1, h, p, c).wait_send()
+
+        if four:
+            for at, which, slot, to in ((1, 0, 0, 3), (2, 1, 0, 3), (3, 0, 1, 2), (3, 1, 1, 2)):
+                pl.when(c == at)(forward(which, h, to, slot).wait_send)
 
         loop(0, n_ctx * per, arrived)
         loop(1, n_mem, sent_mem)
@@ -325,19 +419,15 @@
             owner_copy(h, m, c, lax.rem(m, per), col0).wait_send()
 
     loop(0, heads, finish)
+    both(lambda which: loop(1, n_mem, lambda d: piece(which, lax.rem(m + d, n_mem), m).wait_send()))
+    loop(1, n_ctx, lambda d: relay(lax.rem(c + d, n_ctx), c).wait_send())
     gk_ref[...] = out[0]
     gv_ref[...] = out[1]
 
 
-def hand_on(a, b, c, d, a_out, b_out, c_out, d_out, sem):
-    copies = [
-        pltpu.make_async_copy(src, dst, sem.at[i])
-        for i, (src, dst) in enumerate(((a, a_out), (b, b_out), (c, c_out), (d, d_out)))
-    ]
-    for copy in copies:
-        copy.start()
-    for copy in copies:
-        copy.wait()
+def hand_on(*refs):
+    for src, dst in zip(refs[:4], refs[4:]):
+        dst[...] = src[...]
 
 
 def shards(n_ctx, n_mem, queries, keys, values, out_grad, mem_keys, mem_values, gate_logit, block_ids):
@@ -371,17 +461,18 @@
             pltpu.VMEM((tok, width), F32),
             pltpu.VMEM((n_ctx, tok, width), BF16),
             pltpu.VMEM((n_ctx, tok, width), BF16),
-            pltpu.VMEM((mem_rows, width), BF16),
-            pltpu.VMEM((mem_rows, width), BF16),
+            pltpu.VMEM((2, n_mem, BLOCK, width), BF16),
             pltpu.VMEM((n_ctx, n_mem, rs, width), BF16),
             pltpu.VMEM((n_ctx, n_mem, rs, width), BF16),
             pltpu.VMEM((n_mem, rs, width), BF16),
             pltpu.VMEM((2, BLOCK, columns // n_ctx), BF16),
             pltpu.VMEM((n_ctx, tok, tok), F32),
             pltpu.VMEM((mem_rows // (2 * BLOCK), tok, 2 * BLOCK), F32),
-            dma((8,)),
+            dma((9,)),
             dma((2, heads, n_mem)), dma((2, heads, n_mem)),
-            dma((2, heads, n_ctx)), dma((2, heads, n_ctx)),
+            dma((n_mem,)), dma((n_mem,)),
+            dma((n_ctx,)), dma((n_ctx,)),
+            dma((2, heads, n_ctx)), dma((2, heads, n_ctx)), dma((2, heads)),
             dma((heads, n_ctx)), dma((heads, n_ctx)),
             dma((heads, n_mem)), dma((heads, n_ctx, n_mem // n_ctx)),
         ],
@@ -395,10 +486,8 @@
     return pl.pallas_call(
         hand_on,
         out_shape=tuple(jax.ShapeDtypeStruct(r.shape, r.dtype) for r in results),
-        in_specs=[hbm] * 4,
-        out_specs=(hbm,) * 4,
-        scratch_shapes=[dma((4,))],
-        compiler_params=pltpu.CompilerParams(vmem_limit_bytes=62 * 1024 * 1024),
+        in_specs=[vmem] * 4,
+        out_specs=(vmem,) * 4,
     )(*results)
 
 

time: 123 us -> 95.7 us (0.78)
  Pallas kernels: 121 us -> 94.8 us
    pallas_call x1, Pallas kernels: 40.8 us -> 2.34 us  [shards(): pl.pallas_call(hand_on, out_shape=tuple((jax.ShapeDtypeStruct(r.shape, r....]
    pallas_call x1, Pallas kernels: 80.6 us -> 92.5 us  [shards(): pl.pallas_call(functools.partial(kernel, n_ctx, n_mem), out_shape=(jax.Sh...]
where the time goes in v3:
time: 95.7 us; the launch traced here: 95.5 us
  Pallas kernels  94.8 us (99%)
    pallas_call x1, Pallas kernels, shards(): pl.pallas_call(functools.partial(kernel, n_ctx, n_mem), out_shape=(jax.Sh...  92.5 us
    pallas_call x1, Pallas kernels, shards(): pl.pallas_call(hand_on, out_shape=tuple((jax.ShapeDtypeStruct(r.shape, r....  2.34 us

profile of v3, /device:TPU:3, one launch (start us, length us, event | category | flops | bytes accessed | tf_op | source)
XLA Modules:
  0.0 95.5 jit_solution(17028662507908025089)
XLA Ops:
  0.6 92.5 %shard_map.111 = (bf16[384,512]{1,0:T(8,128)(2,1)}, bf16[384,512]{1,0:T(8,128)(2,1)}, bf16[128,1024]{1,0:T(8,128)(2,1)}, bf16[128,1024]{1,0:T(8,128)(2,1)}) custom-call(s32[3,4]{1,0:T(4,128)} %ids_in.1, f32[4]{0:T(128)} %gate_in.1, bf16[384,512]{1,0:T(8,128)(2,1)} %q_in.1, bf16[384,512]{1,0:T(8,128)(2,1)} %k_ref.1, bf16[384,512]{1,0:T(8,128)(2,1)} %v_ref.1, ...), custom_call_target="tpu_custom_call" | custom-call | flops 3019898880 | bytes 8388608 | tf_op jit(solution)/shard_map/pallas_call | solution.py:443
  93.1 2.3 %shard_map.112 = (bf16[384,512]{1,0:T(8,128)(2,1)}, bf16[384,512]{1,0:T(8,128)(2,1)}, bf16[128,1024]{1,0:T(8,128)(2,1)}, bf16[128,1024]{1,0:T(8,128)(2,1)}) custom-call(bf16[384,512]{1,0:T(8,128)(2,1)} %get-tuple-element.8.refs_0_, bf16[384,512]{1,0:T(8,128)(2,1)} %get-tuple-element.9.refs_1_, bf16[128,1024]{1,0:T(8,128)(2,1)} %get-tuple-element.10.refs_2_, ...), custom_call_target="tpu_custom_call" | custom-call | tf_op jit(solution)/shard_map/pallas_call | solution.py:486

commit v4 on v2

--- a/solution.py
+++ b/solution.py
@@ -145,8 +145,8 @@
     for copy in mine:
         copy.wait()
 
-    difference = (lax.broadcasted_iota(jnp.int32, (tok, tok), 1)
-                  - lax.broadcasted_iota(jnp.int32, (tok, tok), 0))
+    causal = (lax.broadcasted_iota(jnp.int32, (tok, tok), 0)
+              <= lax.broadcasted_iota(jnp.int32, (tok, tok), 1))
 
     def listed(b, r):
         hit = ids[b, 0] == r
@@ -182,13 +182,22 @@
     def share_of_gate(h):
         return 1.0 / (1.0 + jnp.exp(-jnp.full((1, HEAD_SIZE), gate[h], F32)))
 
+    def row_max(s):
+        return jnp.max(s, axis=0, keepdims=True)
+
+    def row_sum(s):
+        return jnp.sum(s, axis=0, keepdims=True)
+
+    def gradient(h, share):
+        return (share * do_ref[:, head(h)].astype(F32))
+
     def local_head(h):
         hc = head(h)
         q = q_ref[:, hc]
-        g = share_of_gate(h)
-        grad = do_ref[:, hc].astype(F32)
-        dl = (1.0 - g) * grad
+        keep = 1.0 - share_of_gate(h)
+        dl = gradient(h, keep)
         dl_low = dl.astype(BF16)
+        dl_t = dl.T
 
         def wait_local(j):
             share(0, h, j, j).wait_recv()
@@ -196,39 +205,42 @@
 
         loop(0, c, wait_local)
 
+        s = jnp.where(causal, dot_nt(kall[c, :, hc], q) * scale2, NEG)
+        s_loc[c] = s
+
         def scores(j, top):
-            s = dot_nt(q, kall[j, :, hc]) * scale2
-            s = jnp.where(difference <= (c - j) * tok, s, NEG)
+            s = dot_nt(kall[j, :, hc], q) * scale2
             s_loc[j] = s
-            return jnp.maximum(top, jnp.max(s, axis=-1, keepdims=True))
-
-        top = lax.fori_loop(0, c + 1, scores, jnp.full((tok, 1), NEG, F32))
+            return jnp.maximum(top, row_max(s))
+
+        top = lax.fori_loop(0, c, scores, row_max(s))
 
         def gather(j, carry):
             total, acc = carry
             e = jnp.exp2(s_loc[j] - top)
             s_loc[j] = e
-            return (total + jnp.sum(e, axis=-1, keepdims=True),
-                    acc + dot_nn(e.astype(BF16), vall[j, :, hc]))
-
-        total, acc = lax.fori_loop(0, c + 1, gather, (jnp.zeros((tok, 1), F32), jnp.zeros((tok, HEAD_SIZE), F32)))
+            return total + row_sum(e), acc + dot_tn(vall[j, :, hc], e.astype(BF16))
+
+        total, acc = lax.fori_loop(0, c + 1, gather, (jnp.zeros((1, tok), F32), jnp.zeros((HEAD_SIZE, tok), F32)))
         inv = 1.0 / total
         local_out = acc * inv
-        delta = jnp.sum(dl * local_out, axis=-1, keepdims=True)
+        delta = row_sum(dl_t * local_out)
 
         def back(j, acc):
-            dp = dot_nt(dl_low, vall[j, :, hc])
+            dp = dot_nt(vall[j, :, hc], dl_low)
             ds = (s_loc[j] * inv) * (dp - delta)
-            return acc + dot_nn(ds.astype(BF16), kall[j, :, hc])
-
-        l_grad[:, hc] = lax.fori_loop(0, c + 1, back, jnp.zeros((tok, HEAD_SIZE), F32))
-        l_out[:, hc] = (1.0 - g) * local_out
+            return acc + dot_tn(kall[j, :, hc], ds.astype(BF16))
+
+        l_grad[rows(h * HEAD_SIZE, HEAD_SIZE), :] = lax.fori_loop(0, c + 1, back, jnp.zeros((HEAD_SIZE, tok), F32))
+        l_out[rows(h * HEAD_SIZE, HEAD_SIZE), :] = keep[:, :1] * local_out
 
     def mem_head(h):
         hc = head(h)
         q = q_ref[:, hc]
         g = share_of_gate(h)
-        grad = do_ref[:, hc].astype(F32)
+        dm = gradient(h, g)
+        dm_low = dm.astype(BF16)
+        dm_t = dm.T
 
         def wait_memory(d):
             p = lax.rem(m + d, n_mem)
@@ -236,48 +248,44 @@
             fetched(1, h, p).wait_recv()
 
         loop(1, n_mem, wait_memory)
-        dm = g * grad
-        dm_low = dm.astype(BF16)
 
         def mem_scores(i, top):
-            s = dot_nt(q, fk[rows(i * chunk, chunk), hc]) * scale2
-            bias = jnp.concatenate(
-                [jnp.concatenate([jnp.full((BLOCK, BLOCK), listed(b, 2 * i + x), F32) for x in range(2)], axis=1)
-                 for b in range(nqb)], axis=0)
-            s = s + bias
+            s = dot_nt(fk[rows(i * chunk, chunk), hc], q) * scale2
+            bias = [jnp.concatenate([jnp.full((1, BLOCK), listed(b, 2 * i + x), F32) for b in range(nqb)], axis=1)
+                    for x in range(2)]
+            s = jnp.concatenate([s[:BLOCK] + bias[0], s[BLOCK:] + bias[1]], axis=0)
             s_mem[i] = s
-            return jnp.maximum(top, jnp.max(s, axis=-1, keepdims=True))
-
-        top2 = lax.fori_loop(0, n_chunk, mem_scores, jnp.full((tok, 1), NEG, F32))
+            return jnp.maximum(top, row_max(s))
+
+        top = lax.fori_loop(0, n_chunk, mem_scores, jnp.full((1, tok), NEG, F32))
 
         def mem_gather(i, carry):
             total, acc = carry
-            e = jnp.exp2(s_mem[i] - top2)
+            e = jnp.exp2(s_mem[i] - top)
             s_mem[i] = e
-            return (total + jnp.sum(e, axis=-1, keepdims=True),
-                    acc + dot_nn(e.astype(BF16), fv[rows(i * chunk, chunk), hc]))
-
-        total2, acc2 = lax.fori_loop(0, n_chunk, mem_gather,
-                                     (jnp.zeros((tok, 1), F32), jnp.zeros((tok, HEAD_SIZE), F32)))
-        inv2 = 1.0 / total2
-        mem_out = acc2 * inv2
-        m_out[:, hc] = g * mem_out
-        delta2 = jnp.sum(dm * mem_out, axis=-1, keepdims=True)
+            return total + row_sum(e), acc + dot_tn(fv[rows(i * chunk, chunk), hc], e.astype(BF16))
+
+        total, acc = lax.fori_loop(0, n_chunk, mem_gather,
+                                   (jnp.zeros((1, tok), F32), jnp.zeros((HEAD_SIZE, tok), F32)))
+        inv = 1.0 / total
+        mem_out = acc * inv
+        m_out[rows(h * HEAD_SIZE, HEAD_SIZE), :] = g[:, :1] * mem_out
+        delta = row_sum(dm_t * mem_out)
 
         def mem_back(i, acc):
-            dw = dot_nt(dm_low, fv[rows(i * chunk, chunk), hc])
-            w = s_mem[i] * inv2
-            ds = (w * (dw - delta2)).astype(BF16)
-            part_k = (dot_tn(ds, q) * scale).astype(BF16)
-            part_v = dot_tn(w.astype(BF16), dm_low).astype(BF16)
+            dw = dot_nt(fv[rows(i * chunk, chunk), hc], dm_low)
+            w = s_mem[i] * inv
+            ds = (w * (dw - delta)).astype(BF16)
+            part_k = (dot_nn(ds, q) * scale).astype(BF16)
+            part_v = dot_nn(w.astype(BF16), dm_low).astype(BF16)
             for x in range(2):
                 for s in range(nsub):
                     at = slice(x * BLOCK + s * rs, x * BLOCK + (s + 1) * rs)
                     parts[s, 2 * i + x, :, hc] = part_k[at]
                     parts[nsub + s, 2 * i + x, :, hc] = part_v[at]
-            return acc + dot_nn(ds, fk[rows(i * chunk, chunk), hc])
-
-        m_grad[:, hc] = lax.fori_loop(0, n_chunk, mem_back, jnp.zeros((tok, HEAD_SIZE), F32))
+            return acc + dot_tn(fk[rows(i * chunk, chunk), hc], ds)
+
+        m_grad[rows(h * HEAD_SIZE, HEAD_SIZE), :] = lax.fori_loop(0, n_chunk, mem_back, jnp.zeros((HEAD_SIZE, tok), F32))
         loop(1, n_ctx, lambda d: part(h, lax.rem(c + d, n_ctx), c).start())
 
     def one_head(h):
@@ -294,8 +302,8 @@
     loop(0, heads, one_head)
     local_head(heads - 1)
     reduce_head(heads - 1)
-    mixed_ref[...] = (m_out[...] + l_out[...]).astype(BF16)
-    qg_ref[...] = ((m_grad[...] + l_grad[...]) * scale).astype(BF16)
+    mixed_ref[...] = (m_out[...] + l_out[...]).T.astype(BF16)
+    qg_ref[...] = ((m_grad[...] + l_grad[...]) * scale).T.astype(BF16)
 
     def finish(h):
         def arrived(t):
@@ -329,15 +337,9 @@
     gv_ref[...] = out[1]
 
 
-def hand_on(a, b, c, d, a_out, b_out, c_out, d_out, sem):
-    copies = [
-        pltpu.make_async_copy(src, dst, sem.at[i])
-        for i, (src, dst) in enumerate(((a, a_out), (b, b_out), (c, c_out), (d, d_out)))
-    ]
-    for copy in copies:
-        copy.start()
-    for copy in copies:
-        copy.wait()
+def hand_on(*refs):
+    for src, dst in zip(refs[:4], refs[4:]):
+        dst[...] = src[...]
 
 
 def shards(n_ctx, n_mem, queries, keys, values, out_grad, mem_keys, mem_values, gate_logit, block_ids):
@@ -365,10 +367,10 @@
             pltpu.SMEM(gate_logit.shape, F32),
             pltpu.VMEM((tok, width), BF16),
             pltpu.VMEM((tok, width), BF16),
-            pltpu.VMEM((tok, width), F32),
-            pltpu.VMEM((tok, width), F32),
-            pltpu.VMEM((tok, width), F32),
-            pltpu.VMEM((tok, width), F32),
+            pltpu.VMEM((width, tok), F32),
+            pltpu.VMEM((width, tok), F32),
+            pltpu.VMEM((width, tok), F32),
+            pltpu.VMEM((width, tok), F32),
             pltpu.VMEM((n_ctx, tok, width), BF16),
             pltpu.VMEM((n_ctx, tok, width), BF16),
             pltpu.VMEM((mem_rows, width), BF16),
@@ -378,7 +380,7 @@
             pltpu.VMEM((n_mem, rs, width), BF16),
             pltpu.VMEM((2, BLOCK, columns // n_ctx), BF16),
             pltpu.VMEM((n_ctx, tok, tok), F32),
-            pltpu.VMEM((mem_rows // (2 * BLOCK), tok, 2 * BLOCK), F32),
+            pltpu.VMEM((mem_rows // (2 * BLOCK), 2 * BLOCK, tok), F32),
             dma((8,)),
             dma((2, heads, n_mem)), dma((2, heads, n_mem)),
             dma((2, heads, n_ctx)), dma((2, heads, n_ctx)),
@@ -395,10 +397,8 @@
     return pl.pallas_call(
         hand_on,
         out_shape=tuple(jax.ShapeDtypeStruct(r.shape, r.dtype) for r in results),
-        in_specs=[hbm] * 4,
-        out_specs=(hbm,) * 4,
-        scratch_shapes=[dma((4,))],
-        compiler_params=pltpu.CompilerParams(vmem_limit_bytes=62 * 1024 * 1024),
+        in_specs=[vmem] * 4,
+        out_specs=(vmem,) * 4,
     )(*results)
 
 

time: 123 us -> 84.3 us (0.69)
  the two profiles are of different devices: /device:TPU:3 before, /device:TPU:7 now
where the time goes in v4:
time: 84.3 us; the launch traced here: 84.1 us
  Pallas kernels  83.5 us (99%)
    pallas_call x1, Pallas kernels, shards(): pl.pallas_call(functools.partial(kernel, n_ctx, n_mem), out_shape=(jax.Sh...  81.2 us
    pallas_call x1, Pallas kernels, shards(): pl.pallas_call(hand_on, out_shape=tuple((jax.ShapeDtypeStruct(r.shape, r....  2.34 us

profile of v4, /device:TPU:7, one launch (start us, length us, event | category | flops | bytes accessed | tf_op | source)
XLA Modules:
  0.0 84.1 jit_solution(418613505307678968)
XLA Ops:
  0.6 81.2 %shard_map.111 = (bf16[384,512]{1,0:T(8,128)(2,1)}, bf16[384,512]{1,0:T(8,128)(2,1)}, bf16[128,1024]{1,0:T(8,128)(2,1)}, bf16[128,1024]{1,0:T(8,128)(2,1)}) custom-call(s32[3,4]{1,0:T(4,128)} %ids_in.1, f32[4]{0:T(128)} %gate_in.1, bf16[384,512]{1,0:T(8,128)(2,1)} %q_in.1, bf16[384,512]{1,0:T(8,128)(2,1)} %k_ref.1, bf16[384,512]{1,0:T(8,128)(2,1)} %v_ref.1, ...), custom_call_target="tpu_custom_call" | custom-call | flops 3019898880 | bytes 8388608 | tf_op jit(solution)/shard_map/pallas_call | solution.py:355
  81.8 2.3 %shard_map.112 = (bf16[384,512]{1,0:T(8,128)(2,1)}, bf16[384,512]{1,0:T(8,128)(2,1)}, bf16[128,1024]{1,0:T(8,128)(2,1)}, bf16[128,1024]{1,0:T(8,128)(2,1)}) custom-call(bf16[384,512]{1,0:T(8,128)(2,1)} %get-tuple-element.8.refs_0_, bf16[384,512]{1,0:T(8,128)(2,1)} %get-tuple-element.9.refs_1_, bf16[128,1024]{1,0:T(8,128)(2,1)} %get-tuple-element.10.refs_2_, ...), custom_call_target="tpu_custom_call" | custom-call | tf_op jit(solution)/shard_map/pallas_call | solution.py:397

commit v5 on v4

--- a/solution.py
+++ b/solution.py
@@ -39,7 +39,7 @@
 def kernel(n_ctx, n_mem, ids_in, gate_in, q_in, k_ref, v_ref, do_in, mk_ref, mv_ref,
            mixed_ref, qg_ref, gk_ref, gv_ref,
            ids, gate, q_ref, do_ref, l_out, l_grad, m_out, m_grad, kall, vall, fk, fv, parts, recv, red, out, s_loc, s_mem,
-           own_sem, fsend, frecv, lsend, lrecv, psend, precv, osend, orecv):
+           own_sem, fsend, frecv, lsend, lrecv, wsend, psend, precv, osend, orecv):
     c = lax.axis_index("ctx")
     m = lax.axis_index("mem")
     tok, width = q_in.shape
@@ -55,6 +55,7 @@
     scale2 = scale * math.log2(math.e)
     chunk = 2 * BLOCK
     n_chunk = n_mem * BLOCK // chunk
+    four = n_ctx == 4
 
     def head(h, base=0):
         return pl.ds(pl.multiple_of(base + h * HEAD_SIZE, HEAD_SIZE), HEAD_SIZE)
@@ -115,6 +116,25 @@
             send_sem=lsend.at[which, h, p], recv_sem=lrecv.at[which, h, slot],
             device_id={"ctx": p, "mem": m}, device_id_type=MESH)
 
+    def forward(which, h, p, slot):
+        buf = (kall, vall)[which]
+        return pltpu.make_async_remote_copy(
+            src_ref=buf.at[slot, :, head(h)], dst_ref=buf.at[slot, :, head(h)],
+            send_sem=wsend.at[which, h], recv_sem=lrecv.at[which, h, slot],
+            device_id={"ctx": p, "mem": m}, device_id_type=MESH)
+
+    def apart(p):
+        return c + p != 3 if four else p >= 0
+
+    ways = ((1, 0, 0, 3), (2, 1, 0, 3), (3, 0, 1, 2), (3, 1, 1, 2)) if four else ()
+
+    def pass_on(h):
+        for at, which, slot, to in ways:
+            @pl.when(c == at)
+            def _(which=which, slot=slot, to=to):
+                share(which, h, slot, slot).wait_recv()
+                forward(which, h, to, slot).start()
+
     def part(h, p, slot):
         return pltpu.make_async_remote_copy(
             src_ref=parts.at[p, :, :, head(h)], dst_ref=recv.at[slot, :, :, head(h)],
@@ -135,8 +155,10 @@
             fetch(1, h, p).start()
 
         def to_ctx(p):
-            share(0, h, p, c).start()
-            share(1, h, p, c).start()
+            @pl.when(apart(p))
+            def _():
+                share(0, h, p, c).start()
+                share(1, h, p, c).start()
 
         loop(c + 1, n_ctx, to_ctx)
         loop(1, n_mem, to_mem)
@@ -200,8 +222,12 @@
         dl_t = dl.T
 
         def wait_local(j):
-            share(0, h, j, j).wait_recv()
-            share(1, h, j, j).wait_recv()
+            for which in range(2):
+                if four:
+                    ahead = jnp.logical_or(jnp.logical_and(c == 1 + which, j == 0), jnp.logical_and(c == 3, j == 1))
+                    pl.when(jnp.logical_not(ahead))(share(which, h, j, j).wait_recv)
+                else:
+                    share(which, h, j, j).wait_recv()
 
         loop(0, c, wait_local)
 
@@ -291,14 +317,16 @@
     def one_head(h):
         @pl.when(h < heads - 1)
         def _():
-            local_head(h)
+            pass_on(h + 1)
 
         mem_head(h)
 
         @pl.when(h > 0)
         def _():
+            local_head(h - 1)
             reduce_head(h - 1)
 
+    pass_on(0)
     loop(0, heads, one_head)
     local_head(heads - 1)
     reduce_head(heads - 1)
@@ -320,8 +348,13 @@
             owner_copy(h, p, c, lax.rem(m, per), col0).wait_send()
 
         def sent_ctx(p):
-            share(0, h, p, c).wait_send()
-            share(1, h, p, c).wait_send()
+            @pl.when(apart(p))
+            def _():
+                share(0, h, p, c).wait_send()
+                share(1, h, p, c).wait_send()
+
+        for at, which, slot, to in ways:
+            pl.when(c == at)(forward(which, h, to, slot).wait_send)
 
         loop(0, n_ctx * per, arrived)
         loop(1, n_mem, sent_mem)
@@ -383,7 +416,7 @@
             pltpu.VMEM((mem_rows // (2 * BLOCK), 2 * BLOCK, tok), F32),
             dma((8,)),
             dma((2, heads, n_mem)), dma((2, heads, n_mem)),
-            dma((2, heads, n_ctx)), dma((2, heads, n_ctx)),
+            dma((2, heads, n_ctx)), dma((2, heads, n_ctx)), dma((2, heads)),
             dma((heads, n_ctx)), dma((heads, n_ctx)),
             dma((heads, n_mem)), dma((heads, n_ctx, n_mem // n_ctx)),
         ],

time: 84.3 us -> 81.8 us (0.970)
  the two profiles are of different devices: /device:TPU:7 before, /device:TPU:3 now
where the time goes in v5:
time: 81.8 us; the launch traced here: 81.6 us
  Pallas kernels  81 us (99%)
    pallas_call x1, Pallas kernels, shards(): pl.pallas_call(functools.partial(kernel, n_ctx, n_mem), out_shape=(jax.Sh...  78.6 us
    pallas_call x1, Pallas kernels, shards(): pl.pallas_call(hand_on, out_shape=tuple((jax.ShapeDtypeStruct(r.shape, r....  2.34 us

profile of v5, /device:TPU:3, one launch (start us, length us, event | category | flops | bytes accessed | tf_op | source)
XLA Modules:
  0.0 81.6 jit_solution(7516083986531762483)
XLA Ops:
  0.6 78.6 %shard_map.111 = (bf16[384,512]{1,0:T(8,128)(2,1)}, bf16[384,512]{1,0:T(8,128)(2,1)}, bf16[128,1024]{1,0:T(8,128)(2,1)}, bf16[128,1024]{1,0:T(8,128)(2,1)}) custom-call(s32[3,4]{1,0:T(4,128)} %ids_in.1, f32[4]{0:T(128)} %gate_in.1, bf16[384,512]{1,0:T(8,128)(2,1)} %q_in.1, bf16[384,512]{1,0:T(8,128)(2,1)} %k_ref.1, bf16[384,512]{1,0:T(8,128)(2,1)} %v_ref.1, ...), custom_call_target="tpu_custom_call" | custom-call | flops 3019898880 | bytes 8388608 | tf_op jit(solution)/shard_map/pallas_call | solution.py:388
  79.3 2.3 %shard_map.112 = (bf16[384,512]{1,0:T(8,128)(2,1)}, bf16[384,512]{1,0:T(8,128)(2,1)}, bf16[128,1024]{1,0:T(8,128)(2,1)}, bf16[128,1024]{1,0:T(8,128)(2,1)}) custom-call(bf16[384,512]{1,0:T(8,128)(2,1)} %get-tuple-element.8.refs_0_, bf16[384,512]{1,0:T(8,128)(2,1)} %get-tuple-element.9.refs_1_, bf16[128,1024]{1,0:T(8,128)(2,1)} %get-tuple-element.10.refs_2_, ...), custom_call_target="tpu_custom_call" | custom-call | tf_op jit(solution)/shard_map/pallas_call | solution.py:430

commit v6 on v5

--- a/solution.py
+++ b/solution.py
@@ -320,16 +320,11 @@
             pass_on(h + 1)
 
         mem_head(h)
-
-        @pl.when(h > 0)
-        def _():
-            local_head(h - 1)
-            reduce_head(h - 1)
+        local_head(h)
+        reduce_head(h)
 
     pass_on(0)
     loop(0, heads, one_head)
-    local_head(heads - 1)
-    reduce_head(heads - 1)
     mixed_ref[...] = (m_out[...] + l_out[...]).T.astype(BF16)
     qg_ref[...] = ((m_grad[...] + l_grad[...]) * scale).T.astype(BF16)
 

time: 81.8 us -> 89.3 us (1.092)
  Pallas kernels: 81 us -> 88.6 us
    pallas_call x1, Pallas kernels: 78.6 us -> 86.2 us  [shards(): pl.pallas_call(functools.partial(kernel, n_ctx, n_mem), out_shape=(jax.Sh...]
where the time goes in v6:
time: 89.3 us; the launch traced here: 89.2 us
  Pallas kernels  88.6 us (99%)
    pallas_call x1, Pallas kernels, shards(): pl.pallas_call(functools.partial(kernel, n_ctx, n_mem), out_shape=(jax.Sh...  86.2 us
    pallas_call x1, Pallas kernels, shards(): pl.pallas_call(hand_on, out_shape=tuple((jax.ShapeDtypeStruct(r.shape, r....  2.34 us

profile of v6, /device:TPU:3, one launch (start us, length us, event | category | flops | bytes accessed | tf_op | source)
XLA Modules:
  0.0 89.2 jit_solution(6598636104243722124)
XLA Ops:
  0.6 86.2 %shard_map.111 = (bf16[384,512]{1,0:T(8,128)(2,1)}, bf16[384,512]{1,0:T(8,128)(2,1)}, bf16[128,1024]{1,0:T(8,128)(2,1)}, bf16[128,1024]{1,0:T(8,128)(2,1)}) custom-call(s32[3,4]{1,0:T(4,128)} %ids_in.1, f32[4]{0:T(128)} %gate_in.1, bf16[384,512]{1,0:T(8,128)(2,1)} %q_in.1, bf16[384,512]{1,0:T(8,128)(2,1)} %k_ref.1, bf16[384,512]{1,0:T(8,128)(2,1)} %v_ref.1, ...), custom_call_target="tpu_custom_call" | custom-call | flops 3019898880 | bytes 8388608 | tf_op jit(solution)/shard_map/pallas_call | solution.py:383
  86.9 2.3 %shard_map.112 = (bf16[384,512]{1,0:T(8,128)(2,1)}, bf16[384,512]{1,0:T(8,128)(2,1)}, bf16[128,1024]{1,0:T(8,128)(2,1)}, bf16[128,1024]{1,0:T(8,128)(2,1)}) custom-call(bf16[384,512]{1,0:T(8,128)(2,1)} %get-tuple-element.8.refs_0_, bf16[384,512]{1,0:T(8,128)(2,1)} %get-tuple-element.9.refs_1_, bf16[128,1024]{1,0:T(8,128)(2,1)} %get-tuple-element.10.refs_2_, ...), custom_call_target="tpu_custom_call" | custom-call | tf_op jit(solution)/shard_map/pallas_call | solution.py:425

commit v7 on v5

--- a/solution.py
+++ b/solution.py
@@ -324,10 +324,15 @@
         @pl.when(h > 0)
         def _():
             local_head(h - 1)
-            reduce_head(h - 1)
+
+        @pl.when(h > 1)
+        def _():
+            reduce_head(h - 2)
 
     pass_on(0)
     loop(0, heads, one_head)
+    if heads > 1:
+        reduce_head(heads - 2)
     local_head(heads - 1)
     reduce_head(heads - 1)
     mixed_ref[...] = (m_out[...] + l_out[...]).T.astype(BF16)

time: 81.8 us -> 82.8 us (1.012)
  Pallas kernels: 81 us -> 82 us
    pallas_call x1, Pallas kernels: 78.6 us -> 79.7 us  [shards(): pl.pallas_call(functools.partial(kernel, n_ctx, n_mem), out_shape=(jax.Sh...]
where the time goes in v7:
time: 82.8 us; the launch traced here: 82.7 us
  Pallas kernels  82 us (99%)
    pallas_call x1, Pallas kernels, shards(): pl.pallas_call(functools.partial(kernel, n_ctx, n_mem), out_shape=(jax.Sh...  79.7 us
    pallas_call x1, Pallas kernels, shards(): pl.pallas_call(hand_on, out_shape=tuple((jax.ShapeDtypeStruct(r.shape, r....  2.34 us

profile of v7, /device:TPU:3, one launch (start us, length us, event | category | flops | bytes accessed | tf_op | source)
XLA Modules:
  0.0 82.7 jit_solution(14424579213924917305)
XLA Ops:
  0.6 79.7 %shard_map.111 = (bf16[384,512]{1,0:T(8,128)(2,1)}, bf16[384,512]{1,0:T(8,128)(2,1)}, bf16[128,1024]{1,0:T(8,128)(2,1)}, bf16[128,1024]{1,0:T(8,128)(2,1)}) custom-call(s32[3,4]{1,0:T(4,128)} %ids_in.1, f32[4]{0:T(128)} %gate_in.1, bf16[384,512]{1,0:T(8,128)(2,1)} %q_in.1, bf16[384,512]{1,0:T(8,128)(2,1)} %k_ref.1, bf16[384,512]{1,0:T(8,128)(2,1)} %v_ref.1, ...), custom_call_target="tpu_custom_call" | custom-call | flops 3019898880 | bytes 8388608 | tf_op jit(solution)/shard_map/pallas_call | solution.py:393
  80.3 2.3 %shard_map.112 = (bf16[384,512]{1,0:T(8,128)(2,1)}, bf16[384,512]{1,0:T(8,128)(2,1)}, bf16[128,1024]{1,0:T(8,128)(2,1)}, bf16[128,1024]{1,0:T(8,128)(2,1)}) custom-call(bf16[384,512]{1,0:T(8,128)(2,1)} %get-tuple-element.8.refs_0_, bf16[384,512]{1,0:T(8,128)(2,1)} %get-tuple-element.9.refs_1_, bf16[128,1024]{1,0:T(8,128)(2,1)} %get-tuple-element.10.refs_2_, ...), custom_call_target="tpu_custom_call" | custom-call | tf_op jit(solution)/shard_map/pallas_call | solution.py:435

commit v8 on v5

--- a/solution.py
+++ b/solution.py
@@ -160,8 +160,8 @@
                 share(0, h, p, c).start()
                 share(1, h, p, c).start()
 
+        loop(1, n_mem, to_mem)
         loop(c + 1, n_ctx, to_ctx)
-        loop(1, n_mem, to_mem)
 
     loop(0, heads, start_head)
     for copy in mine:

time: 81.8 us -> 81.8 us (level)
  no operation moved by 1% of the time
where the time goes in v8:
time: 81.8 us; the launch traced here: 81.6 us
  Pallas kernels  81 us (99%)
    pallas_call x1, Pallas kernels, shards(): pl.pallas_call(functools.partial(kernel, n_ctx, n_mem), out_shape=(jax.Sh...  78.6 us
    pallas_call x1, Pallas kernels, shards(): pl.pallas_call(hand_on, out_shape=tuple((jax.ShapeDtypeStruct(r.shape, r....  2.34 us

profile of v8, /device:TPU:3, one launch (start us, length us, event | category | flops | bytes accessed | tf_op | source)
XLA Modules:
  0.0 81.6 jit_solution(17658269759241151690)
XLA Ops:
  0.6 78.6 %shard_map.111 = (bf16[384,512]{1,0:T(8,128)(2,1)}, bf16[384,512]{1,0:T(8,128)(2,1)}, bf16[128,1024]{1,0:T(8,128)(2,1)}, bf16[128,1024]{1,0:T(8,128)(2,1)}) custom-call(s32[3,4]{1,0:T(4,128)} %ids_in.1, f32[4]{0:T(128)} %gate_in.1, bf16[384,512]{1,0:T(8,128)(2,1)} %q_in.1, bf16[384,512]{1,0:T(8,128)(2,1)} %k_ref.1, bf16[384,512]{1,0:T(8,128)(2,1)} %v_ref.1, ...), custom_call_target="tpu_custom_call" | custom-call | flops 3019898880 | bytes 8388608 | tf_op jit(solution)/shard_map/pallas_call | solution.py:388
  79.3 2.3 %shard_map.112 = (bf16[384,512]{1,0:T(8,128)(2,1)}, bf16[384,512]{1,0:T(8,128)(2,1)}, bf16[128,1024]{1,0:T(8,128)(2,1)}, bf16[128,1024]{1,0:T(8,128)(2,1)}) custom-call(bf16[384,512]{1,0:T(8,128)(2,1)} %get-tuple-element.8.refs_0_, bf16[384,512]{1,0:T(8,128)(2,1)} %get-tuple-element.9.refs_1_, bf16[128,1024]{1,0:T(8,128)(2,1)} %get-tuple-element.10.refs_2_, ...), custom_call_target="tpu_custom_call" | custom-call | tf_op jit(solution)/shard_map/pallas_call | solution.py:430
